TPU v7x, 512 devices: a whole 4x8x8 slice. The times are simulated.
512 devices in a mesh: dp: 32 (over y, x), fsdp: 16 (over z, core).
Axes of the slice: x: 4, y: 8, z: 8, core: 2. Of those that a mesh axis runs over, the one named last changes fastest.
Arguments:
- grad: bfloat16 [32, 2048, 4096], P('dp', 'fsdp'), may hold values from -8 to 8
- error: bfloat16 [32, 2048, 4096], P('dp', 'fsdp'), may hold values from -3 to 3
- q_warm: float32 [64, 4096], P(None, 'fsdp'), may hold values from -5 to 5
Outputs:
- error_next: bfloat16 [32, 2048, 4096], P('dp', 'fsdp')
- decompressed: bfloat16 [2048, 4096], P('fsdp', 'dp')
- q_next: float32 [64, 4096], P(None, 'fsdp')
All inputs are finite; a program needn't handle non-finite values.
Results may differ from a plain program's by a relative error of at most 0.0074.
Values may be sent and summed in bfloat16 or wider, within the bound.
No kernel may reach another device: no remote copies, remote signals or barrier semaphores. Data moves between devices by JAX's collectives and lax.ppermute only.
A program may use at most 64 MiB of HBM per device.

v0:
```python
import jax
import jax.numpy as jnp
from jax import lax
from jax.sharding import PartitionSpec as P


def on_device(grad, error, q_warm):
    col_count = grad.shape[2]
    dp_count = lax.axis_size("dp")
    merged = (grad[0].astype(jnp.float32) + error[0].astype(jnp.float32)).astype(jnp.bfloat16)
    merged = lax.optimization_barrier(merged)
    warm_bf = q_warm.astype(jnp.bfloat16)
    columns = merged
    partial_p = lax.dot_general(
        columns,
        lax.all_gather(warm_bf, "fsdp", axis=1, tiled=True),
        (((1,), (1,)), ((), ())),
        preferred_element_type=jnp.float32,
    )
    p_mean = lax.psum(partial_p, "dp") / dp_count
    gram_local = jnp.dot(p_mean.T, p_mean, precision=lax.Precision.HIGHEST)
    gram_matrix = lax.psum(gram_local, "fsdp")
    chol_lower = jnp.linalg.cholesky(gram_matrix)
    p_ortho = lax.linalg.triangular_solve(
        chol_lower, p_mean, left_side=False, lower=True, transpose_a=True
    )
    ortho_bf = p_ortho.astype(jnp.bfloat16)
    q_terms = lax.dot_general(
        ortho_bf, merged, (((0,), (0,)), ((), ())), preferred_element_type=jnp.float32
    )
    q_share = lax.psum_scatter(q_terms, "fsdp", scatter_dimension=1, tiled=True)
    q_next = lax.psum(q_share, "dp") / dp_count
    q_bf = q_next.astype(jnp.bfloat16)
    columns = merged
    approx = jnp.dot(
        ortho_bf,
        lax.all_gather(q_bf, "fsdp", axis=1, tiled=True),
        preferred_element_type=jnp.float32,
    )
    fresh = (columns.astype(jnp.float32) - approx).astype(jnp.bfloat16)
    rebuilt = jnp.stack([fresh, approx.astype(jnp.bfloat16)])
    error_next = rebuilt[0][None]
    slice_cols = col_count // dp_count
    decompressed = lax.dynamic_slice_in_dim(
        rebuilt[1], lax.axis_index("dp") * slice_cols, slice_cols, 1
    )
    return (error_next, decompressed, q_next)


def solution(mesh):
    return jax.shard_map(
        on_device,
        mesh=mesh,
        in_specs=(P("dp", "fsdp", None), P("dp", "fsdp", None), P(None, "fsdp")),
        out_specs=(P("dp", "fsdp", None), P("fsdp", "dp"), P(None, "fsdp")),
        check_vma=False,
    )
```

profile of v0, /device:TPU:1, one launch (start us, length us, event | category | flops | bytes accessed | tf_op | source)
XLA Modules:
  0.0 473.2 jit_solution(11881098142726556848)
XLA Ops:
  7.2 0.0 copy-start
  7.2 0.0 reduce-scatter.2.cloned.1.call-start
  7.2 1.8 fusion
  9.0 0.0 copy-done
  9.0 25.9 %all_gather.6 = bf16[64,4096]{1,0:T(8,128)(2,1)S(1)} all-gather(bf16[64,256]{1,0:T(8,128)(2,1)S(1)} %convert_element_type.37), channel_id=1, replica_groups=mesh['dp'=32,'fsdp'=16] {'fsdp'}, dimensions={1}, use_global_device_ids=true | all-gather | bytes 557056 | tf_op jit(solution)/shard_map/all_gather | solution.py:16
  35.0 0.5 fusion.13
  35.5 115.8 %psum.21 = f32[128,64]{0,1:T(8,128)S(1)} all-reduce(f32[128,64]{0,1:T(8,128)S(1)} %fusion.13), channel_id=1, replica_groups=mesh['dp'=32,'fsdp'=16] {'dp'}, use_global_device_ids=true, to_apply=%region_0.0 | all-reduce | flops 8192 | bytes 65536 | tf_op jit(solution)/shard_map/psum | solution.py:20
  151.3 0.2 fusion.6
  151.5 69.8 %psum.22 = f32[64,64]{0,1:T(8,128)S(1)} all-reduce(f32[64,64]{0,1:T(8,128)S(1)} %fusion.6), channel_id=1, replica_groups=mesh['dp'=32,'fsdp'=16] {'fsdp'}, use_global_device_ids=true, to_apply=%region_1.0 | all-reduce | flops 4096 | bytes 32768 | tf_op jit(solution)/shard_map/psum | solution.py:22
  221.3 0.1 copy.7
  221.4 5.8 %cholesky.16 = f32[64,64]{1,0:T(8,128)S(1)} custom-call(f32[64,64]{1,0:T(8,128)S(1)} %fusion.4), custom_call_target="Cholesky" | custom-call | tf_op jit(solution)/shard_map/jit(cholesky)/cholesky | solution.py:23
  227.3 0.6 compare_reduce_fusion
  227.9 0.7 fusion.2
  228.6 4.9 %custom-call.6 = f32[1,64,64]{1,2,0:T(8,128)S(1)} custom-call(f32[1,64,64]{2,1,0:T(8,128)S(1)} %fusion.2), custom_call_target="InvertDiagBlocksLowerTriangular" | custom-call | tf_op jit(solution)/shard_map/triangular_solve | solution.py:24
  233.5 0.3 convolution_convert_fusion
  233.7 1.3 fusion.14
  235.0 0.0 reduce-scatter.2.cloned.1.call-update
  235.0 0.0 all-reduce.2.cloned.1.call-start
  235.1 52.5 %reduce-scatter.2.cloned.1.call-done = f32[64,256]{1,0:T(8,128)} async-done(((f32[64,4096]{1,0:T(8,128)}), f32[64,256]{1,0:T(8,128)}) %reduce-scatter.2.cloned.1.call-update) | async-done | bytes 65552 | tf_op jit(solution)/shard_map/reduce_scatter | solution.py:31
  287.6 0.0 all-reduce.2.cloned.1.call-update
  287.6 150.9 %all-reduce.2.cloned.1.call-done = f32[64,256]{1,0:T(8,128)} async-done(((f32[64,256]{1,0:T(8,128)}), f32[64,256]{1,0:T(8,128)}) %all-reduce.2.cloned.1.call-update) | async-done | bytes 65552 | tf_op jit(solution)/shard_map/psum | solution.py:32
  438.5 1.5 fusion.12
  440.0 24.0 %all_gather.7 = bf16[64,4096]{1,0:T(8,128)(2,1)S(1)} all-gather(bf16[64,256]{1,0:T(8,128)(2,1)S(1)} %get-tuple-element.3), channel_id=1, replica_groups=mesh['dp'=32,'fsdp'=16] {'fsdp'}, dimensions={1}, use_global_device_ids=true | all-gather | bytes 557056 | tf_op jit(solution)/shard_map/all_gather | solution.py:37
  464.0 0.5 fusion.15
  464.5 1.2 fusion.1
  465.7 0.6 dynamic-slice_convert_fusion
  (3 shorter events, 0.0 us)
Async XLA Ops:
  7.2 1.9 copy-start
  7.2 280.4 %reduce-scatter.2.cloned.1.call-start = ((), (), s32[]{:S(2)}) async-start(), calls=%async_computation.1 | async-start | bytes 1114112 | tf_op jit(solution)/shard_map/reduce_scatter | solution.py:31
  235.0 203.5 %all-reduce.2.cloned.1.call-start = ((), (), s32[]{:S(2)}) async-start(), calls=%async_computation.2 | async-start | bytes 131072 | tf_op jit(solution)/shard_map/psum | solution.py:32
Sparse Core Ops, SparseCore 0:
  235.2 52.3 reduce-scatter.1
  291.4 147.0 all-reduce.1
where the time goes:
time: 473 us
  blocking collectives  236 us (50%)
  waiting for transfers between devices  203 us (43%)
  other arithmetic  16.6 us (4%)
  between operations  14.1 us (3%)
    psum x1, waiting for transfers between devices, on_device(): q_next = lax.psum(q_share, 'dp') / dp_count  151 us
    psum x1, blocking collectives, on_device(): p_mean = lax.psum(partial_p, 'dp') / dp_count  116 us
    psum x1, blocking collectives, on_device(): gram_matrix = lax.psum(gram_local, 'fsdp')  69.8 us
    reduce_scatter x1, waiting for transfers between devices, on_device(): q_share = lax.psum_scatter(q_terms, 'fsdp', scatter_dimension=1, tiled=True)  52.5 us
    all_gather x1, blocking collectives, on_device(): lax.all_gather(warm_bf, 'fsdp', axis=1, tiled=True)  25.9 us
    all_gather x1, blocking collectives, on_device(): lax.all_gather(q_bf, 'fsdp', axis=1, tiled=True)  24 us
  transfers between devices with their start and end apart: 2, of which 2 were waited for; matrix products, arithmetic and copies ran while one was open for 0% of the time, Pallas kernels for 0%

commit v1 on v0

v1 whole, which is shorter than its diff:
```python
import jax
import jax.numpy as jnp
from jax import lax
from jax.sharding import Mesh, PartitionSpec as P

Y, X, Z, CORES = 8, 4, 8, 2
DP = ("y", "x")
FSDP = ("z", "core")
EXACT = lax.Precision.HIGHEST


def copies_to_all(value, axis, count):
    return lax.all_to_all(jnp.broadcast_to(value[None], (count,) + value.shape), axis, 0, 0)


def on_device(grad, error, q_warm):
    rows, col_count = grad.shape[1:]
    rank = q_warm.shape[0]
    dp_count = Y * X
    cols = col_count // dp_count
    merged = (grad[0].astype(jnp.float32) + error[0].astype(jnp.float32)).astype(jnp.bfloat16)
    merged = lax.optimization_barrier(merged)

    by_column = merged.reshape(rows, dp_count, cols).transpose(1, 0, 2)
    landed = lax.all_to_all(by_column, DP, 0, 0)

    warm = lax.all_gather(q_warm.astype(jnp.bfloat16), FSDP, axis=1, tiled=True)
    left = lax.dot_general(
        warm, merged, (((1,), (1,)), ((), ())), preferred_element_type=jnp.float32
    )
    left = copies_to_all(left, "x", X).sum(0)
    left = copies_to_all(left, "y", Y).sum(0) / dp_count

    mean_cols = landed.astype(jnp.float32).sum(0) / dp_count
    q_terms = jnp.dot(left, mean_cols, precision=EXACT)
    gram = lax.dot_general(left, left, (((1,), (1,)), ((), ())), precision=EXACT)
    both = jnp.concatenate([q_terms, gram], axis=1)
    both = lax.psum(both, "core")
    both = copies_to_all(both, "z", Z).sum(0)
    q_sum, gram = both[:, :cols], both[:, cols:]

    chol_lower = jnp.linalg.cholesky(gram)
    inverse = lax.linalg.triangular_solve(
        chol_lower, jnp.eye(rank, dtype=jnp.float32), left_side=True, lower=True
    )
    q_mine = jnp.dot(inverse, q_sum, precision=EXACT).astype(jnp.bfloat16)
    q_all = copies_to_all(q_mine, DP, dp_count)
    ortho = jnp.dot(inverse, left, precision=EXACT).astype(jnp.bfloat16)
    q_bf = q_all.transpose(1, 0, 2).reshape(rank, col_count)

    def rebuild(right):
        return lax.dot_general(
            ortho, right, (((0,), (0,)), ((), ())), preferred_element_type=jnp.float32
        )

    decompressed = rebuild(q_mine).astype(jnp.bfloat16)
    error_next = (merged.astype(jnp.float32) - rebuild(q_bf)).astype(jnp.bfloat16)[None]
    shard = col_count // (Z * CORES)
    q_next = lax.dynamic_slice_in_dim(q_bf, lax.axis_index(FSDP) * shard, shard, 1)
    return (error_next, decompressed, q_next.astype(jnp.float32))


def solution(mesh):
    grid = Mesh(mesh.devices.reshape(Y, X, Z, CORES), DP + FSDP)
    return jax.shard_map(
        on_device,
        mesh=grid,
        in_specs=(P(DP, FSDP, None), P(DP, FSDP, None), P(None, FSDP)),
        out_specs=(P(DP, FSDP, None), P(FSDP, DP), P(None, FSDP)),
        check_vma=False,
    )
```

time: 473 us -> 151 us (0.32)
  blocking collectives: 236 us -> 62.7 us
  waiting for transfers between devices: 203 us -> 48.2 us
  starting transfers between devices: 0.08 us -> 16.5 us
  between operations: 14.1 us -> 0.82 us
    psum x2 -> x1, blocking collectives: 186 us -> 7.75 us  [on_device(): both = lax.psum(both, 'core')]
    psum x1 -> x0, waiting for transfers between devices: 151 us -> none  [on_device(): q_next = lax.psum(q_share, 'dp') / dp_count]
    reduce_scatter x1 -> x0, waiting for transfers between devices: 52.5 us -> none  [on_device(): q_share = lax.psum_scatter(q_terms, 'fsdp', scatter_dimension=1, tiled=True)]
    all_to_all x0 -> x3, waiting for transfers between devices: none -> 48.2 us  [the longest x1 24.6 us: on_device(): landed = lax.all_to_all(by_column, DP, 0, 0)]
    all_to_all x0 -> x2, blocking collectives: none -> 29 us  [copies_to_all(): lax.all_to_all(jnp.broadcast_to(value[None], (count,) + value.shape), axi...]
    all_gather x2 -> x1, blocking collectives: 49.9 us -> 25.9 us  [on_device(): warm = lax.all_gather(q_warm.astype(jnp.bfloat16), FSDP, axis=1, tiled=True)]
    all_to_all x0 -> x3, starting transfers between devices: none -> 16.5 us  [the longest x2 12 us: copies_to_all(): lax.all_to_all(jnp.broadcast_to(value[None], (count,) + value.shape), axi...]
    another operation x6 -> x5, other arithmetic: 13.3 us -> 12.1 us  [the longest x3 6.52 us: on_device(): chol_lower = jnp.linalg.cholesky(gram)]
  transfers between devices with their start and end apart: 2 -> 3, of which waited for: 2 -> 3; matrix products, arithmetic and copies ran while one was open for 0% -> 2% of each run, Pallas kernels for 0% -> 0%
where the time goes in v1:
time: 151 us; the launch traced here: 150 us
  blocking collectives  62.7 us (42%)
  waiting for transfers between devices  48.2 us (32%)
  starting transfers between devices  16.5 us (11%)
  other arithmetic  14.8 us (10%)
  matrix products  3.65 us (2%)
  local copies, waits for them, and re-layouts  3.08 us (2%)
    all_to_all x2, blocking collectives, copies_to_all(): lax.all_to_all(jnp.broadcast_to(value[None], (count,) + value.shape), axi...  29 us
    all_gather x1, blocking collectives, on_device(): warm = lax.all_gather(q_warm.astype(jnp.bfloat16), FSDP, axis=1, tiled=True)  25.9 us
    all_to_all x1, waiting for transfers between devices, on_device(): landed = lax.all_to_all(by_column, DP, 0, 0)  24.6 us
    all_to_all x2, waiting for transfers between devices, copies_to_all(): lax.all_to_all(jnp.broadcast_to(value[None], (count,) + value.shape), axi...  23.6 us
    all_to_all x2, starting transfers between devices, copies_to_all(): lax.all_to_all(jnp.broadcast_to(value[None], (count,) + value.shape), axi...  12 us
    psum x1, blocking collectives, on_device(): both = lax.psum(both, 'core')  7.75 us
    another operation x3, other arithmetic, on_device(): chol_lower = jnp.linalg.cholesky(gram)  6.52 us
    another operation x2, other arithmetic, on_device(): lax.linalg.triangular_solve(chol_lower, jnp.eye(rank, dtype=jnp.float32),...  5.55 us
  transfers between devices with their start and end apart: 3, of which 3 were waited for; matrix products, arithmetic and copies ran while one was open for 2% of the time, Pallas kernels for 0%

profile of v1, /device:TPU:1, one launch (start us, length us, event | category | flops | bytes accessed | tf_op | source)
XLA Modules:
  0.0 149.7 jit_solution(2842579236053540615)
XLA Ops:
  0.6 0.0 copy-start
  0.6 1.8 %fusion.2 = bf16[128,4096]{1,0:T(8,128)(2,1)S(1)} fusion(bf16[1,128,4096]{2,1,0:T(8,128)(2,1)} %param.4, bf16[1,128,4096]{2,1,0:T(8,128)(2,1)} %param.3), kind=kLoop, calls=%fused_computation.9 | loop fusion | flops 2097152 | bytes 3145728 | tf_op jit(solution)/shard_map/convert_element_type | solution.py:21
  2.5 0.0 copy-done
  2.5 25.9 %all_gather.3 = bf16[64,4096]{1,0:T(8,128)(2,1)S(1)} all-gather(bf16[64,256]{1,0:T(8,128)(2,1)S(1)} %convert_element_type.44), channel_id=1, replica_groups=mesh['y'=8,'x'=4,'z'=8,'core'=2] {'z','core'}, dimensions={1}, use_global_device_ids=true | all-gather | bytes 557056 | tf_op jit(solution)/shard_map/all_gather | solution.py:27
  28.4 0.5 convolution_bitcast_fusion
  29.0 8.6 %all_to_all.25 = f32[4,64,128]{2,1,0:T(8,128)S(1)} all-to-all(f32[4,64,128]{2,1,0:T(8,128)S(1)} %broadcast_in_dim.11), channel_id=1, replica_groups=mesh['y'=8,'x'=4,'z'=8,'core'=2] {'x'}, dimensions={0} | all-to-all | bytes 262144 | tf_op jit(solution)/shard_map/all_to_all | solution.py:13
  37.6 0.7 broadcast_in_dim.12
  38.3 6.8 %all-to-all-start.1 = ((f32[8,64,128]{2,1,0:T(8,128)}), f32[8,64,128]{2,1,0:T(8,128)S(1)}, u32[]{:S(2)}, u32[]{:S(2)}) async-start(f32[8,64,128]{2,1,0:T(8,128)} %broadcast_in_dim.12), calls=%async_computation.1 | async-start | bytes 524288 | tf_op jit(solution)/shard_map/all_to_all | solution.py:13
  45.1 1.3 bitcast_bitcast_fusion
  46.4 8.0 %all-to-all-done.1 = f32[8,64,128]{2,1,0:T(8,128)S(1)} async-done(((f32[8,64,128]{2,1,0:T(8,128)}), f32[8,64,128]{2,1,0:T(8,128)S(1)}, u32[]{:S(2)}, u32[]{:S(2)}) %all-to-all-start.1) | async-done | bytes 262176 | tf_op jit(solution)/shard_map/all_to_all | solution.py:13
  54.4 4.5 %all-to-all-start.2 = ((bf16[32,128,128]{2,1,0:T(8,128)(2,1)}), bf16[32,128,128]{2,1,0:T(8,128)(2,1)S(1)}, u32[]{:S(2)}, u32[]{:S(2)}) async-start(bf16[32,128,128]{2,1,0:T(8,128)(2,1)} %bitcast_bitcast_fusion), calls=%async_computation.2 | async-start | bytes 2097152 | tf_op jit(solution)/shard_map/all_to_all | solution.py:25
  59.0 0.2 fusion.12
  59.2 24.6 %all-to-all-done.2 = bf16[32,128,128]{2,1,0:T(8,128)(2,1)S(1)} async-done(((bf16[32,128,128]{2,1,0:T(8,128)(2,1)}), bf16[32,128,128]{2,1,0:T(8,128)(2,1)S(1)}, u32[]{:S(2)}, u32[]{:S(2)}) %all-to-all-start.2) | async-done | bytes 1048608 | tf_op jit(solution)/shard_map/all_to_all | solution.py:25
  83.8 0.2 convert_reduce_fusion
  83.9 0.2 fusion.3
  84.2 7.7 %psum.7 = f32[64,192]{1,0:T(8,128)S(1)} all-reduce(f32[64,192]{1,0:T(8,128)S(1)} %pad_maximum_fusion), channel_id=1, replica_groups=mesh['y'=8,'x'=4,'z'=8,'core'=2] {'core'}, use_global_device_ids=true, to_apply=%region_3.0 | all-reduce | flops 12288 | bytes 98304 | tf_op jit(solution)/shard_map/psum | solution.py:38
  91.9 20.4 %all_to_all.26 = f32[8,64,192]{2,1,0:T(8,128)S(1)} all-to-all(f32[8,64,192]{2,1,0:T(8,128)S(1)} %broadcast_in_dim.14), channel_id=1, replica_groups=mesh['y'=8,'x'=4,'z'=8,'core'=2] {'z'}, dimensions={0} | all-to-all | bytes 786432 | tf_op jit(solution)/shard_map/all_to_all | solution.py:13
  112.4 0.1 copy.16
  112.5 5.8 %cholesky.17 = f32[64,64]{1,0:T(8,128)S(1)} custom-call(f32[64,64]{1,0:T(8,128)S(1)} %fusion.9), custom_call_target="Cholesky" | custom-call | tf_op jit(solution)/shard_map/jit(cholesky)/cholesky | solution.py:42
  118.4 0.6 compare_reduce_fusion
  119.0 0.7 fusion.5
  119.7 4.9 %custom-call.6 = f32[1,64,64]{1,2,0:T(8,128)S(1)} custom-call(f32[1,64,64]{2,1,0:T(8,128)S(1)} %fusion.5), custom_call_target="InvertDiagBlocksLowerTriangular" | custom-call | tf_op jit(solution)/shard_map/triangular_solve | solution.py:43
  124.6 0.2 fusion.7
  124.8 0.2 convolution_convert_fusion.1
  125.0 0.9 broadcast_in_dim.15
  125.9 5.1 %all-to-all-start.4 = ((bf16[32,64,128]{2,1,0:T(8,128)(2,1)}), bf16[32,64,128]{2,1,0:T(8,128)(2,1)S(1)}, u32[]{:S(2)}, u32[]{:S(2)}) async-start(bf16[32,64,128]{2,1,0:T(8,128)(2,1)} %broadcast_in_dim.15), calls=%async_computation.4 | async-start | bytes 1048576 | tf_op jit(solution)/shard_map/all_to_all | solution.py:13
  131.0 0.2 convolution_convert_fusion.2
  131.2 0.8 convolution_convert_fusion
  132.0 15.6 %all-to-all-done.4 = bf16[32,64,128]{2,1,0:T(8,128)(2,1)S(1)} async-done(((bf16[32,64,128]{2,1,0:T(8,128)(2,1)}), bf16[32,64,128]{2,1,0:T(8,128)(2,1)S(1)}, u32[]{:S(2)}, u32[]{:S(2)}) %all-to-all-start.4) | async-done | bytes 524320 | tf_op jit(solution)/shard_map/all_to_all | solution.py:13
  147.6 0.1 copy_bitcast_fusion
  147.6 0.6 dynamic-slice_convert_fusion
  148.3 1.4 fusion.1
  (10 shorter events, 0.2 us)
Async XLA Ops:
  0.6 1.8 %copy-start = (f32[64,256]{1,0:T(8,128)S(1)}, f32[64,256]{1,0:T(8,128)}, u32[]{:S(2)}) copy-start(f32[64,256]{1,0:T(8,128)} %param.5) | copy-start | bytes 196612
  38.3 16.1 %all-to-all-start.1 = ((f32[8,64,128]{2,1,0:T(8,128)}), f32[8,64,128]{2,1,0:T(8,128)S(1)}, u32[]{:S(2)}, u32[]{:S(2)}) async-start(f32[8,64,128]{2,1,0:T(8,128)} %broadcast_in_dim.12), calls=%async_computation.1 | async-start | bytes 524288 | tf_op jit(solution)/shard_map/all_to_all | solution.py:13
  54.4 29.4 %all-to-all-start.2 = ((bf16[32,128,128]{2,1,0:T(8,128)(2,1)}), bf16[32,128,128]{2,1,0:T(8,128)(2,1)S(1)}, u32[]{:S(2)}, u32[]{:S(2)}) async-start(bf16[32,128,128]{2,1,0:T(8,128)(2,1)} %bitcast_bitcast_fusion), calls=%async_computation.2 | async-start | bytes 2097152 | tf_op jit(solution)/shard_map/all_to_all | solution.py:25
  125.9 21.7 %all-to-all-start.4 = ((bf16[32,64,128]{2,1,0:T(8,128)(2,1)}), bf16[32,64,128]{2,1,0:T(8,128)(2,1)S(1)}, u32[]{:S(2)}, u32[]{:S(2)}) async-start(bf16[32,64,128]{2,1,0:T(8,128)(2,1)} %broadcast_in_dim.15), calls=%async_computation.4 | async-start | bytes 1048576 | tf_op jit(solution)/shard_map/all_to_all | solution.py:13

commit v2 on v1

v2 whole, which is shorter than its diff:
```python
import jax
import jax.numpy as jnp
from jax import lax
from jax.experimental import pallas as pl
from jax.experimental.pallas import tpu as pltpu
from jax.sharding import Mesh, PartitionSpec as P

Y, X, Z, CORES = 8, 4, 8, 2
DP = ("y", "x")
FSDP = ("z", "core")
EXACT = lax.Precision.HIGHEST
F32, BF16 = jnp.float32, jnp.bfloat16
VMEM = pl.BlockSpec(memory_space=pltpu.VMEM)
SMEM = pl.BlockSpec(memory_space=pltpu.SMEM)
PARAMS = pltpu.CompilerParams(vmem_limit_bytes=32 * 1024 * 1024)
RANK = 64


def call(kernel, out, *operands, scalars=0):
    specs = [SMEM] * scalars + [VMEM] * (len(operands) - scalars)
    many = isinstance(out, (list, tuple))
    return pl.pallas_call(
        kernel,
        out_shape=out,
        in_specs=specs,
        out_specs=[VMEM] * len(out) if many else VMEM,
        compiler_params=PARAMS,
    )(*operands)


def shape(dtype, *dims):
    return jax.ShapeDtypeStruct(dims, dtype)


def left_kernel(landed_ref, warm_ref, out_ref):
    _, rows, col_count = landed_ref.shape
    wide = col_count // Y
    stacked = landed_ref[...].reshape(X * rows, col_count)
    every = lax.dot_general(
        stacked, warm_ref[...], (((1,), (1,)), ((), ())), preferred_element_type=F32
    )
    left = every[:rows]
    for x in range(1, X):
        left = left + every[x * rows : (x + 1) * rows]
    high = left.astype(BF16)
    rest = left - high.astype(F32)
    middle = rest.astype(BF16)
    low = (rest - middle.astype(F32)).astype(BF16)
    first = jnp.concatenate([high, middle], axis=1)
    second = jnp.concatenate([low, jnp.zeros_like(low)], axis=1)
    for y in range(Y):
        span = pl.ds(y * wide, wide)
        total = landed_ref[0, :, span].astype(F32)
        for x in range(1, X):
            total = total + landed_ref[x, :, span].astype(F32)
        out_ref[y, :, :wide] = total.astype(BF16)
        out_ref[y, :, wide : wide + 2 * RANK] = first
        out_ref[y, :, wide + 2 * RANK :] = second


def terms_kernel(landed_ref, out_ref):
    total = landed_ref[0].astype(F32)
    for y in range(1, Y):
        total = total + landed_ref[y].astype(F32)
    wide = total.shape[1] - 4 * RANK
    total = total * (1.0 / (X * Y))
    mean = total[:, :wide]
    left = (
        total[:, wide : wide + RANK]
        + total[:, wide + RANK : wide + 2 * RANK]
        + total[:, wide + 2 * RANK : wide + 3 * RANK]
    )
    over_rows = (((0,), (0,)), ((), ()))
    q_terms = lax.dot_general(left, mean, over_rows, precision=EXACT, preferred_element_type=F32)
    gram = lax.dot_general(left, left, over_rows, precision=EXACT, preferred_element_type=F32)
    cols = wide // X
    half, quarter = RANK // 2, RANK // 4
    rows = left.shape[0] // 2
    folded_left = jnp.concatenate([left[:rows], left[rows:]], axis=1)
    for core in range(CORES):
        own = gram[core * half : (core + 1) * half]
        folded = jnp.concatenate([own[:quarter], own[quarter:]], axis=1)
        for x in range(X):
            peer = x * CORES + core
            out_ref[peer, :half] = q_terms[core * half : (core + 1) * half, x * cols : (x + 1) * cols]
            out_ref[peer, half : half + quarter] = folded
            out_ref[peer, half + quarter :] = folded_left


def factor_kernel(where_ref, sums_ref, left_ref, q_ref, ortho_ref):
    half, quarter = RANK // 2, RANK // 4
    lane = lax.broadcasted_iota(jnp.int32, (8, 2 * RANK), 1)
    sub = lax.broadcasted_iota(jnp.int32, (8, 2 * RANK), 0)
    blocks = []
    for b in range(RANK // 8):
        core, at = divmod(b, 4)
        raw = sums_ref[core, half + 8 * (at % 2) : half + 8 * (at % 2) + 8, :]
        if at >= 2:
            raw = pltpu.roll(raw, RANK, 1)
        unit = (lane == sub + RANK + 8 * b).astype(F32)
        blocks.append(jnp.where(lane < RANK, raw, unit))

    def lane_copy(value, column):
        return jnp.broadcast_to(value[:, column : column + 1], value.shape)

    def row_copy(value, row):
        return jnp.broadcast_to(value[row : row + 1], value.shape)

    inverse_rows = []
    for b in range(RANK // 8):
        here = blocks[b]
        columns = [lane_copy(here, 8 * b + j) for j in range(8)]
        later = [
            [lane_copy(blocks[t], 8 * b + j) for j in range(8)] for t in range(b + 1, RANK // 8)
        ]
        scales = jnp.zeros_like(here)
        for j in range(8):
            pivot = row_copy(columns[j], j)
            recip = 1.0 / pivot
            scales = jnp.where(sub == j, recip, scales)
            factor = jnp.where(sub > j, columns[j] * recip, 0.0)
            here = here - factor * row_copy(here, j)
            for other in range(j + 1, 8):
                columns[other] = columns[other] - factor * row_copy(columns[other], j)
        inverse_rows.append(here * jnp.sqrt(scales))
        if b + 1 == RANK // 8:
            break
        solved = here * scales
        uppers = [columns[j] * scales for j in range(8)]
        for j in range(7, 0, -1):
            factor = jnp.where(sub < j, uppers[j], 0.0)
            solved = solved - factor * row_copy(solved, j)
        for t in range(b + 1, RANK // 8):
            update = later[t - b - 1][0] * row_copy(solved, 0)
            for j in range(1, 8):
                update = update + later[t - b - 1][j] * row_copy(solved, j)
            blocks[t] = blocks[t] - update
    inverse = jnp.concatenate(inverse_rows, axis=0)[:, RANK:]

    q_sum = jnp.concatenate([sums_ref[0, :half], sums_ref[1, :half]], axis=0)
    q_mine = jnp.dot(inverse, q_sum, precision=EXACT, preferred_element_type=F32).astype(BF16)
    for peer in range(q_ref.shape[0]):
        q_ref[peer] = q_mine
    core = where_ref[2]
    pieces = []
    for x in range(X):
        piece = left_ref[x * CORES + core, half + quarter :]
        pieces += [piece[:, :RANK], piece[:, RANK:]]
    left = jnp.concatenate(pieces, axis=0)
    ortho_ref[...] = lax.dot_general(
        left, inverse, (((1,), (1,)), ((), ())), precision=EXACT, preferred_element_type=F32
    ).astype(BF16)


def rebuild_kernel(where_ref, q_ref, ortho_ref, merged_ref, error_ref, own_ref, q_next_ref):
    ortho = ortho_ref[...]
    count, _, cols = q_ref.shape
    for d in range(count):
        span = pl.ds(d * cols, cols)
        approx = jnp.dot(ortho, q_ref[d], preferred_element_type=F32)
        error_ref[0, :, span] = (merged_ref[:, span].astype(F32) - approx).astype(BF16)
    own_ref[...] = jnp.dot(ortho, q_ref[where_ref[0]], preferred_element_type=F32).astype(BF16)
    each = q_next_ref.shape[1] // cols
    for i in range(each):
        q_next_ref[:, i * cols : (i + 1) * cols] = q_ref[where_ref[1] * each + i].astype(F32)


def on_device(grad, error, q_warm):
    rows, col_count = grad.shape[1:]
    dp_count = Y * X
    cols = col_count // dp_count
    wide = col_count // Y
    part = rows // X
    merged = (grad[0].astype(F32) + error[0].astype(F32)).astype(BF16)
    merged = lax.optimization_barrier(merged)

    landed = lax.all_to_all(merged.reshape(X, part, col_count), "x", 0, 0)
    warm = lax.all_gather(q_warm.astype(BF16), FSDP, axis=1, tiled=True)
    to_y = call(left_kernel, shape(BF16, Y, part, wide + 4 * RANK), landed, warm)
    to_pair = call(
        terms_kernel, shape(F32, X * CORES, RANK, cols), lax.all_to_all(to_y, "y", 0, 0)
    )
    landed = lax.all_to_all(to_pair, ("x", "core"), 0, 0)
    kept = RANK // 2 + RANK // 4
    sums = landed[:, :kept].sum(0)
    sums = lax.all_to_all(jnp.broadcast_to(sums[None], (Z,) + sums.shape), "z", 0, 0).sum(0)
    sums = lax.all_gather(sums, "core")

    where = jnp.stack([lax.axis_index(DP), lax.axis_index(FSDP), lax.axis_index("core")])
    q_copies, ortho = call(
        factor_kernel,
        (shape(BF16, dp_count, RANK, cols), shape(BF16, rows, RANK)),
        where, sums, landed, scalars=1,
    )
    q_all = lax.all_to_all(q_copies, DP, 0, 0)
    return call(
        rebuild_kernel,
        (
            shape(BF16, 1, rows, col_count),
            shape(BF16, rows, cols),
            shape(F32, RANK, q_warm.shape[1]),
        ),
        where, q_all, ortho, merged, scalars=1,
    )


def solution(mesh):
    grid = Mesh(mesh.devices.reshape(Y, X, Z, CORES), DP + FSDP)
    return jax.shard_map(
        on_device,
        mesh=grid,
        in_specs=(P(DP, FSDP, None), P(DP, FSDP, None), P(None, FSDP)),
        out_specs=(P(DP, FSDP, None), P(FSDP, DP), P(None, FSDP)),
        check_vma=False,
    )
```

time: 151 us -> 111 us (0.74)
  waiting for transfers between devices: 48.2 us -> 8.51 us
  blocking collectives: 62.7 us -> 82.6 us
  other arithmetic: 14.8 us -> 2.89 us
  starting transfers between devices: 16.5 us -> 8.37 us
  Pallas kernels: 0 us -> 6.97 us
  matrix products: 3.65 us -> 0 us
  local copies, waits for them, and re-layouts: 3.08 us -> 0.69 us
    all_to_all x3 -> x2, waiting for transfers between devices: 48.2 us -> 8.51 us  [the longest x1 8.51 us: on_device(): lax.all_to_all(jnp.broadcast_to(sums[None], (Z,) + sums.shape), 'z', 0, 0)]
    all_to_all x2 -> x3, blocking collectives: 29 us -> 53 us  [the longest x1 21 us: on_device(): lax.all_to_all(to_y, 'y', 0, 0)]
    another operation x5 -> x1, other arithmetic: 12.1 us -> 0.08 us  [on_device(): jnp.stack([lax.axis_index(DP), lax.axis_index(FSDP), lax.axis_index('core...]
    all_to_all x3 -> x2, starting transfers between devices: 16.5 us -> 8.37 us  [the longest x1 4.97 us: on_device(): landed = lax.all_to_all(merged.reshape(X, part, col_count), 'x', 0, 0)]
    psum x1 -> x0, blocking collectives: 7.75 us -> none  [on_device(): both = lax.psum(both, 'core')]
    pallas_call x0 -> x4, Pallas kernels: none -> 6.97 us  [call(): pl.pallas_call(kernel, out_shape=out, in_specs=specs, out_specs=[VMEM] *...]
    all_gather x1 -> x2, blocking collectives: 25.9 us -> 29.6 us  [the longest x1 25.4 us: on_device(): warm = lax.all_gather(q_warm.astype(BF16), FSDP, axis=1, tiled=True)]
    dot_general x7 -> x0, matrix products: 3.42 us -> none  [the longest x2 2.23 us: rebuild(): lax.dot_general(ortho, right, (((0,), (0,)), ((), ())), preferred_element...]
  transfers between devices with their start and end apart: 3 -> 2, of which waited for: 3 -> 1; matrix products, arithmetic and copies ran while one was open for 2% -> 0% of each run, Pallas kernels for 0% -> 0%
where the time goes in v2:
time: 111 us
  blocking collectives  82.6 us (74%)
  waiting for transfers between devices  8.51 us (8%)
  starting transfers between devices  8.37 us (8%)
  Pallas kernels  6.97 us (6%)
  other arithmetic  2.89 us (3%)
    all_gather x1, blocking collectives, on_device(): warm = lax.all_gather(q_warm.astype(BF16), FSDP, axis=1, tiled=True)  25.4 us
    all_to_all x1, blocking collectives, on_device(): lax.all_to_all(to_y, 'y', 0, 0)  21 us
    all_to_all x1, blocking collectives, on_device(): q_all = lax.all_to_all(q_copies, DP, 0, 0)  19.6 us
    all_to_all x1, blocking collectives, on_device(): landed = lax.all_to_all(to_pair, ('x', 'core'), 0, 0)  12.3 us
    all_to_all x1, waiting for transfers between devices, on_device(): lax.all_to_all(jnp.broadcast_to(sums[None], (Z,) + sums.shape), 'z', 0, 0)  8.51 us
    pallas_call x4, Pallas kernels, call(): pl.pallas_call(kernel, out_shape=out, in_specs=specs, out_specs=[VMEM] *...  6.97 us
    all_to_all x1, starting transfers between devices, on_device(): landed = lax.all_to_all(merged.reshape(X, part, col_count), 'x', 0, 0)  4.97 us
    all_gather x1, blocking collectives, on_device(): sums = lax.all_gather(sums, 'core')  4.24 us
  transfers between devices with their start and end apart: 2, of which 1 were waited for; matrix products, arithmetic and copies ran while one was open for 0% of the time, Pallas kernels for 0%

profile of v2, /device:TPU:1, one launch (start us, length us, event | category | flops | bytes accessed | tf_op | source)
XLA Modules:
  0.0 110.7 jit_solution(16135877343545636975)
XLA Ops:
  0.6 2.8 %fusion.merged_ref = bf16[128,4096]{1,0:T(8,128)(2,1)} fusion(bf16[1,128,4096]{2,1,0:T(8,128)(2,1)} %param.4, bf16[1,128,4096]{2,1,0:T(8,128)(2,1)} %param.3), kind=kLoop, calls=%fused_computation.1 | loop fusion | flops 2097152 | bytes 3145728 | tf_op jit(solution)/shard_map/convert_element_type | solution.py:174
  3.4 0.0 copy-start
  3.4 5.0 %all-to-all-start = ((bf16[4,32,4096]{2,1,0:T(8,128)(2,1)}), bf16[4,32,4096]{2,1,0:T(8,128)(2,1)S(1)}, u32[]{:S(2)}, u32[]{:S(2)}) async-start(bf16[4,32,4096]{2,1,0:T(8,128)(2,1)} %bitcast.4), calls=%async_computation | async-start | bytes 2097152 | tf_op jit(solution)/shard_map/all_to_all | solution.py:177
  8.4 0.0 copy-done
  8.4 25.4 %all_gather.9.warm_ref = bf16[64,4096]{1,0:T(8,128)(2,1)S(1)} all-gather(bf16[64,256]{1,0:T(8,128)(2,1)S(1)} %convert_element_type.21), channel_id=1, replica_groups=mesh['y'=8,'x'=4,'z'=8,'core'=2] {'z','core'}, dimensions={1}, use_global_device_ids=true | all-gather | bytes 557056 | tf_op jit(solution)/shard_map/all_gather | solution.py:178
  33.8 0.0 all-to-all-done.landed_ref
  33.8 0.5 shard_map.58
  34.3 21.0 %all_to_all.25.landed_ref = bf16[8,32,768]{2,1,0:T(8,128)(2,1)S(1)} all-to-all(bf16[8,32,768]{2,1,0:T(8,128)(2,1)S(1)} %shard_map.58), channel_id=1, replica_groups=mesh['y'=8,'x'=4,'z'=8,'core'=2] {'y'}, dimensions={0} | all-to-all | bytes 786432 | tf_op jit(solution)/shard_map/all_to_all | solution.py:181
  55.4 0.5 shard_map.59
  55.8 12.3 %all_to_all.26.left_ref = f32[8,64,128]{2,1,0:T(8,128)S(1)} all-to-all(f32[8,64,128]{2,1,0:T(8,128)S(1)} %shard_map.59), channel_id=1, replica_groups=mesh['y'=8,'x'=4,'z'=8,'core'=2] {'x','core'}, dimensions={0} | all-to-all | bytes 524288 | tf_op jit(solution)/shard_map/all_to_all | solution.py:183
  68.2 0.7 broadcast_in_dim.2
  68.9 3.4 %all-to-all-start.3 = ((f32[8,48,128]{2,1,0:T(8,128)}), f32[8,48,128]{2,1,0:T(8,128)S(1)}, u32[]{:S(2)}, u32[]{:S(2)}) async-start(f32[8,48,128]{2,1,0:T(8,128)} %broadcast_in_dim.2), calls=%async_computation.3 | async-start | bytes 393216 | tf_op jit(solution)/shard_map/all_to_all | solution.py:186
  72.3 0.1 pad_add_fusion.where_ref
  72.4 8.5 %all-to-all-done.3 = f32[8,48,128]{2,1,0:T(8,128)S(1)} async-done(((f32[8,48,128]{2,1,0:T(8,128)}), f32[8,48,128]{2,1,0:T(8,128)S(1)}, u32[]{:S(2)}, u32[]{:S(2)}) %all-to-all-start.3) | async-done | bytes 196640 | tf_op jit(solution)/shard_map/all_to_all | solution.py:186
  80.9 4.2 %all-gather = f32[96,128]{1,0:T(8,128)S(1)} all-gather(f32[48,128]{1,0:T(8,128)S(1)} %reduce_sum.19), channel_id=2, replica_groups=mesh['y'=8,'x'=4,'z'=8,'core'=2] {'core'}, dimensions={0}, use_global_device_ids=true | all-gather | bytes 73728 | tf_op jit(solution)/shard_map/all_gather | solution.py:187
  85.2 3.3 %shard_map.60 = (bf16[32,64,128]{2,1,0:T(8,128)(2,1)S(1)}, bf16[128,64]{1,0:T(8,128)(2,1)S(1)}) custom-call(s32[3]{0:T(128)S(1)} %pad_add_fusion.where_ref, f32[2,48,128]{2,1,0:T(8,128)S(1)} %bitcast.7, f32[8,64,128]{2,1,0:T(8,128)S(1)} %all_to_all.26.left_ref), custom_call_target="tpu_custom_call" | custom-call | tf_op jit(solution)/shard_map/pallas_call | solution.py:22
  88.4 19.6 %all_to_all.27.q_ref = bf16[32,64,128]{2,1,0:T(8,128)(2,1)S(1)} all-to-all(bf16[32,64,128]{2,1,0:T(8,128)(2,1)S(1)} %get-tuple-element.5), channel_id=1, replica_groups=mesh['y'=8,'x'=4,'z'=8,'core'=2] {'y','x'}, dimensions={0} | all-to-all | bytes 1048576 | tf_op jit(solution)/shard_map/all_to_all | solution.py:195
  108.1 2.7 %shard_map.61 = (bf16[1,128,4096]{2,1,0:T(8,128)(2,1)}, bf16[128,128]{1,0:T(8,128)(2,1)}, f32[64,256]{1,0:T(8,128)}) custom-call(s32[3]{0:T(128)S(1)} %pad_add_fusion.where_ref, bf16[32,64,128]{2,1,0:T(8,128)(2,1)S(1)} %all_to_all.27.q_ref, bf16[128,64]{1,0:T(8,128)(2,1)S(1)} %get-tuple-element.6.ortho_ref, bf16[128,4096]{1,0:T(8,128)(2,1)} %fusion.merged_ref), custom_call_target="tpu_custom_call" | custom-call | tf_op jit(solution)/shard_map/pallas_call | solution.py:22
  (3 shorter events, 0.0 us)
Async XLA Ops:
  3.4 5.0 %copy-start = (f32[64,256]{1,0:T(8,128)S(1)}, f32[64,256]{1,0:T(8,128)}, u32[]{:S(2)}) copy-start(f32[64,256]{1,0:T(8,128)} %param.5) | copy-start | bytes 196612
  3.4 30.4 %all-to-all-start = ((bf16[4,32,4096]{2,1,0:T(8,128)(2,1)}), bf16[4,32,4096]{2,1,0:T(8,128)(2,1)S(1)}, u32[]{:S(2)}, u32[]{:S(2)}) async-start(bf16[4,32,4096]{2,1,0:T(8,128)(2,1)} %bitcast.4), calls=%async_computation | async-start | bytes 2097152 | tf_op jit(solution)/shard_map/all_to_all | solution.py:177
  68.9 12.0 %all-to-all-start.3 = ((f32[8,48,128]{2,1,0:T(8,128)}), f32[8,48,128]{2,1,0:T(8,128)S(1)}, u32[]{:S(2)}, u32[]{:S(2)}) async-start(f32[8,48,128]{2,1,0:T(8,128)} %broadcast_in_dim.2), calls=%async_computation.3 | async-start | bytes 393216 | tf_op jit(solution)/shard_map/all_to_all | solution.py:186

commit v3 on v2

v3 whole, which is shorter than its diff:
```python
import jax
import jax.numpy as jnp
from jax import lax
from jax.experimental import pallas as pl
from jax.experimental.pallas import tpu as pltpu
from jax.sharding import Mesh, PartitionSpec as P

YH, YL, X, Z, CORES = 4, 2, 4, 8, 2
NEAR = ("yl", "x")
DP = ("yh", "yl", "x")
FSDP = ("z", "core")
NEARS = YL * X
CUTS = 8
SPANS = 4
REPLICAS = YH * YL * X
RANK = 64
HALF, QUARTER = RANK // 2, RANK // 4
EXACT = lax.Precision.HIGHEST
F32, BF16 = jnp.float32, jnp.bfloat16
VMEM = pl.BlockSpec(memory_space=pltpu.VMEM)
ANY = pl.BlockSpec(memory_space=pl.ANY)
LIMIT = 32 * 1024 * 1024


def call(kernel, out, *operands):
    many = isinstance(out, (list, tuple))
    return pl.pallas_call(
        kernel,
        out_shape=out,
        in_specs=[VMEM] * len(operands),
        out_specs=[VMEM] * len(out) if many else VMEM,
        compiler_params=pltpu.CompilerParams(vmem_limit_bytes=LIMIT),
    )(*operands)


def shape(dtype, *dims):
    return jax.ShapeDtypeStruct(dims, dtype)


def merge_kernel(grad_hbm, error_hbm, merged_hbm, grad, error, merged, in_sems, out_sems):
    part = merged.shape[0] // CUTS
    copies = []
    for i in range(CUTS):
        span = pl.ds(i * part, part)
        copies.append(
            (
                pltpu.make_async_copy(grad_hbm.at[0, span], grad.at[span], in_sems.at[0, i]),
                pltpu.make_async_copy(error_hbm.at[0, span], error.at[span], in_sems.at[1, i]),
                pltpu.make_async_copy(merged.at[span], merged_hbm.at[span], out_sems.at[i]),
            )
        )
        copies[i][0].start()
        copies[i][1].start()
    for i in range(CUTS):
        copies[i][0].wait()
        copies[i][1].wait()
        span = pl.ds(i * part, part)
        merged[span] = (grad[span].astype(F32) + error[span].astype(F32)).astype(BF16)
        copies[i][2].start()
    for i in range(CUTS):
        copies[i][2].wait()


def merge(grad, error):
    _, rows, col_count = grad.shape
    return pl.pallas_call(
        merge_kernel,
        out_shape=shape(BF16, rows, col_count),
        in_specs=[ANY, ANY],
        out_specs=ANY,
        scratch_shapes=[pltpu.VMEM((rows, col_count), BF16)] * 3
        + [pltpu.SemaphoreType.DMA((2, CUTS)), pltpu.SemaphoreType.DMA((CUTS,))],
        compiler_params=pltpu.CompilerParams(vmem_limit_bytes=60 * 1024 * 1024),
    )(grad, error)


def left_kernel(landed_ref, warm_ref, out_ref):
    _, rows, col_count = landed_ref.shape
    wide = col_count // YH
    stacked = landed_ref[...].reshape(NEARS * rows, col_count)
    every = lax.dot_general(
        stacked, warm_ref[...], (((1,), (1,)), ((), ())), preferred_element_type=F32
    )
    left = every[:rows]
    for peer in range(1, NEARS):
        left = left + every[peer * rows : (peer + 1) * rows]
    high = left.astype(BF16)
    rest = left - high.astype(F32)
    middle = rest.astype(BF16)
    low = (rest - middle.astype(F32)).astype(BF16)
    first = jnp.concatenate([high, middle], axis=1)
    second = jnp.concatenate([low, jnp.zeros_like(low)], axis=1)
    for y in range(YH):
        span = pl.ds(y * wide, wide)
        total = landed_ref[0, :, span].astype(F32)
        for peer in range(1, NEARS):
            total = total + landed_ref[peer, :, span].astype(F32)
        out_ref[y, :, :wide] = total.astype(BF16)
        out_ref[y, :, wide : wide + 2 * RANK] = first
        out_ref[y, :, wide + 2 * RANK :] = second


def terms_kernel(landed_ref, out_ref):
    total = landed_ref[0].astype(F32)
    for y in range(1, YH):
        total = total + landed_ref[y].astype(F32)
    wide = total.shape[1] - 4 * RANK
    total = total * (1.0 / REPLICAS)
    mean = total[:, :wide]
    left = (
        total[:, wide : wide + RANK]
        + total[:, wide + RANK : wide + 2 * RANK]
        + total[:, wide + 2 * RANK : wide + 3 * RANK]
    )
    q_terms = lax.dot_general(
        left, mean, (((0,), (0,)), ((), ())), precision=EXACT, preferred_element_type=F32
    )
    cols = wide // NEARS
    rows = left.shape[0] // 2
    folded_left = jnp.concatenate([left[:rows], left[rows:]], axis=1)
    for core in range(CORES):
        for near in range(NEARS):
            peer = near * CORES + core
            span = slice(near * cols, (near + 1) * cols)
            out_ref[peer, :HALF] = q_terms[core * HALF : (core + 1) * HALF, span]
            out_ref[peer, HALF:] = folded_left


def spread_kernel(landed_ref, out_ref, left_ref):
    core = lax.axis_index("core")
    total = landed_ref[0, :HALF]
    for peer in range(1, NEARS * CORES):
        total = total + landed_ref[peer, :HALF]

    def left_of(which):
        pieces = []
        for near in range(NEARS):
            piece = landed_ref[near * CORES + which, HALF:]
            pieces += [piece[:, :RANK], piece[:, RANK:]]
        return jnp.concatenate(pieces, axis=0)

    mine, other = left_of(core), left_of(1 - core)
    left_ref[...] = mine
    both = jnp.concatenate([mine, other], axis=0)
    gram = lax.dot_general(
        both, both, (((0,), (0,)), ((), ())), precision=EXACT, preferred_element_type=F32
    )
    own = jnp.where(core == 0, gram[:HALF], gram[HALF:])
    folded = jnp.concatenate([own[:QUARTER], own[QUARTER:]], axis=1)
    for z in range(Z):
        out_ref[z, :HALF] = total
        out_ref[z, HALF:] = folded


def factor_kernel(landed_ref, left_ref, q_ref, ortho_ref):
    sums = landed_ref[:, 0]
    for z in range(1, Z):
        sums = sums + landed_ref[:, z]
    lane = lax.broadcasted_iota(jnp.int32, (8, 2 * RANK), 1)
    sub = lax.broadcasted_iota(jnp.int32, (8, 2 * RANK), 0)
    blocks = []
    for b in range(RANK // 8):
        core, at = divmod(b, 4)
        raw = sums[core, HALF + 8 * (at % 2) : HALF + 8 * (at % 2) + 8, :]
        if at >= 2:
            raw = pltpu.roll(raw, RANK, 1)
        unit = (lane == sub + RANK + 8 * b).astype(F32)
        blocks.append(jnp.where(lane < RANK, raw, unit))

    def lane_copy(value, column):
        return jnp.broadcast_to(value[:, column : column + 1], value.shape)

    def row_copy(value, row):
        return jnp.broadcast_to(value[row : row + 1], value.shape)

    inverse_rows = []
    for b in range(RANK // 8):
        here = blocks[b]
        columns = [lane_copy(here, 8 * b + j) for j in range(8)]
        later = [
            [lane_copy(blocks[t], 8 * b + j) for j in range(8)] for t in range(b + 1, RANK // 8)
        ]
        scales = jnp.zeros_like(here)
        for j in range(8):
            pivot = row_copy(columns[j], j)
            recip = 1.0 / pivot
            scales = jnp.where(sub == j, recip, scales)
            factor = jnp.where(sub > j, columns[j] * recip, 0.0)
            here = here - factor * row_copy(here, j)
            for other in range(j + 1, 8):
                columns[other] = columns[other] - factor * row_copy(columns[other], j)
        inverse_rows.append(here * jnp.sqrt(scales))
        if b + 1 == RANK // 8:
            break
        solved = here * scales
        uppers = [columns[j] * scales for j in range(8)]
        for j in range(7, 0, -1):
            factor = jnp.where(sub < j, uppers[j], 0.0)
            solved = solved - factor * row_copy(solved, j)
        for t in range(b + 1, RANK // 8):
            update = later[t - b - 1][0] * row_copy(solved, 0)
            for j in range(1, 8):
                update = update + later[t - b - 1][j] * row_copy(solved, j)
            blocks[t] = blocks[t] - update
    inverse = jnp.concatenate(inverse_rows, axis=0)[:, RANK:]

    q_sum = jnp.concatenate([sums[0, :HALF], sums[1, :HALF]], axis=0)
    q_mine = jnp.dot(inverse, q_sum, precision=EXACT, preferred_element_type=F32).astype(BF16)
    core = lax.axis_index("core")
    q_half = jnp.where(core == 0, q_mine[:HALF], q_mine[HALF:])
    for peer in range(q_ref.shape[0]):
        q_ref[peer] = q_half
    ortho_ref[...] = lax.dot_general(
        left_ref[...],
        inverse,
        (((1,), (1,)), ((), ())),
        precision=EXACT,
        preferred_element_type=F32,
    ).astype(BF16)


def rebuild_kernel(
    q_ref, ortho_ref, merged_hbm, error_hbm, own_ref, q_next_ref, q_all, merged, error, in_sems, out_sems
):
    cols = q_ref.shape[3]
    col_count = merged.shape[1]
    wide = col_count // SPANS
    ins, outs = [], []
    for i in range(SPANS):
        span = pl.ds(i * wide, wide)
        ins.append(pltpu.make_async_copy(merged_hbm.at[:, span], merged.at[:, span], in_sems.at[i]))
        outs.append(
            pltpu.make_async_copy(error.at[:, span], error_hbm.at[0, :, span], out_sems.at[i])
        )
        ins[i].start()
    for d in range(REPLICAS):
        q_all[:HALF, d * cols : (d + 1) * cols] = q_ref[0, d]
        q_all[HALF:, d * cols : (d + 1) * cols] = q_ref[1, d]
    ortho = ortho_ref[...]
    for i in range(SPANS):
        span = slice(i * wide, (i + 1) * wide)
        approx = jnp.dot(ortho, q_all[:, span], preferred_element_type=F32)
        ins[i].wait()
        error[:, span] = (merged[:, span].astype(F32) - approx).astype(BF16)
        outs[i].start()

    own = (lax.axis_index("yh") * YL + lax.axis_index("yl")) * X + lax.axis_index("x")
    right = jnp.concatenate([q_ref[0, own], q_ref[1, own]], axis=0)
    own_ref[...] = jnp.dot(ortho, right, preferred_element_type=F32).astype(BF16)
    count = q_next_ref.shape[1] // cols
    first = (lax.axis_index("z") * CORES + lax.axis_index("core")) * count
    for i in range(count):
        q_next_ref[:HALF, i * cols : (i + 1) * cols] = q_ref[0, first + i].astype(F32)
        q_next_ref[HALF:, i * cols : (i + 1) * cols] = q_ref[1, first + i].astype(F32)
    for i in range(SPANS):
        outs[i].wait()


def rebuild(q_all, ortho, merged, shard):
    rows, col_count = merged.shape
    cols = q_all.shape[3]
    return pl.pallas_call(
        rebuild_kernel,
        out_shape=(
            shape(BF16, 1, rows, col_count),
            shape(BF16, rows, cols),
            shape(F32, RANK, shard),
        ),
        in_specs=[VMEM, VMEM, ANY],
        out_specs=[ANY, VMEM, VMEM],
        scratch_shapes=[
            pltpu.VMEM((RANK, col_count), BF16),
            pltpu.VMEM((rows, col_count), BF16),
            pltpu.VMEM((rows, col_count), BF16),
            pltpu.SemaphoreType.DMA((SPANS,)),
            pltpu.SemaphoreType.DMA((SPANS,)),
        ],
        compiler_params=pltpu.CompilerParams(vmem_limit_bytes=LIMIT),
    )(q_all, ortho, merged)


def on_device(grad, error, q_warm):
    rows, col_count = grad.shape[1:]
    cols = col_count // REPLICAS
    wide = col_count // YH
    part = rows // NEARS
    merged = merge(grad, error)

    landed = lax.all_to_all(merged.reshape(NEARS, part, col_count), NEAR, 0, 0)
    warm = lax.all_gather(q_warm.astype(BF16), FSDP, axis=1, tiled=True)
    to_far = call(left_kernel, shape(BF16, YH, part, wide + 4 * RANK), landed, warm)
    landed = lax.all_to_all(to_far, "yh", 0, 0)
    to_near = call(terms_kernel, shape(F32, NEARS * CORES, HALF + part // 2, cols), landed)
    landed = lax.all_to_all(to_near, NEAR + ("core",), 0, 0)
    terms, left = call(
        spread_kernel,
        (shape(F32, Z, HALF + QUARTER, cols), shape(F32, rows, RANK)),
        landed,
    )
    terms = lax.all_gather(lax.all_to_all(terms, "z", 0, 0), "core")
    q_copies, ortho = call(
        factor_kernel,
        (shape(BF16, REPLICAS, HALF, cols), shape(BF16, rows, RANK)),
        terms,
        left,
    )
    q_all = lax.all_gather(lax.all_to_all(q_copies, DP, 0, 0), "core")
    return rebuild(q_all, ortho, merged, q_warm.shape[1])


def solution(mesh):
    grid = Mesh(mesh.devices.reshape(YH, YL, X, Z, CORES), DP + FSDP)
    return jax.shard_map(
        on_device,
        mesh=grid,
        in_specs=(P(DP, FSDP, None), P(DP, FSDP, None), P(None, FSDP)),
        out_specs=(P(DP, FSDP, None), P(FSDP, DP), P(None, FSDP)),
        check_vma=False,
    )
```

time: 111 us -> 106 us (0.955)
  waiting for transfers between devices: 8.51 us -> 0.01 us
  blocking collectives: 82.6 us -> 89.5 us
  other arithmetic: 2.89 us -> 0.01 us
  starting transfers between devices: 8.37 us -> 6.01 us
  Pallas kernels: 6.97 us -> 9.32 us
    all_to_all x2 -> x1, waiting for transfers between devices: 8.51 us -> 0.01 us  [on_device(): landed = lax.all_to_all(merged.reshape(NEARS, part, col_count), NEAR, 0, 0)]
    all_gather x1 -> x2, blocking collectives: 4.24 us -> 8.75 us  [the longest x1 4.64 us: on_device(): terms = lax.all_gather(lax.all_to_all(terms, 'z', 0, 0), 'core')]
    convert_element_type x1 -> x0, other arithmetic: 2.78 us -> none  [on_device(): merged = (grad[0].astype(F32) + error[0].astype(F32)).astype(BF16)]
    all_to_all x2 -> x1, starting transfers between devices: 8.37 us -> 6.01 us  [on_device(): landed = lax.all_to_all(merged.reshape(NEARS, part, col_count), NEAR, 0, 0)]
    all_to_all x3 -> x4, blocking collectives: 53 us -> 55.3 us  [the longest x1 15.6 us: on_device(): q_all = lax.all_gather(lax.all_to_all(q_copies, DP, 0, 0), 'core')]
    pallas_call x4 -> x6, Pallas kernels: 6.97 us -> 9.32 us  [the longest x4 4.31 us: call(): pl.pallas_call(kernel, out_shape=out, in_specs=[VMEM] * len(operands), ou...]
  transfers between devices with their start and end apart: 2 -> 1, of which waited for: 1 -> 0; matrix products, arithmetic and copies ran while one was open for 0% -> 0% of each run, Pallas kernels for 0% -> 0%
where the time goes in v3:
time: 106 us
  blocking collectives  89.5 us (84%)
  Pallas kernels  9.32 us (9%)
  starting transfers between devices  6.01 us (6%)
    all_gather x1, blocking collectives, on_device(): warm = lax.all_gather(q_warm.astype(BF16), FSDP, axis=1, tiled=True)  25.4 us
    all_to_all x1, blocking collectives, on_device(): q_all = lax.all_gather(lax.all_to_all(q_copies, DP, 0, 0), 'core')  15.6 us
    all_to_all x1, blocking collectives, on_device(): landed = lax.all_to_all(to_near, NEAR + ('core',), 0, 0)  15.3 us
    all_to_all x1, blocking collectives, on_device(): landed = lax.all_to_all(to_far, 'yh', 0, 0)  13.5 us
    all_to_all x1, blocking collectives, on_device(): terms = lax.all_gather(lax.all_to_all(terms, 'z', 0, 0), 'core')  11 us
    all_to_all x1, starting transfers between devices, on_device(): landed = lax.all_to_all(merged.reshape(NEARS, part, col_count), NEAR, 0, 0)  6.01 us
    all_gather x1, blocking collectives, on_device(): terms = lax.all_gather(lax.all_to_all(terms, 'z', 0, 0), 'core')  4.64 us
    pallas_call x4, Pallas kernels, call(): pl.pallas_call(kernel, out_shape=out, in_specs=[VMEM] * len(operands), ou...  4.31 us
  transfers between devices with their start and end apart: 1, of which 0 were waited for; matrix products, arithmetic and copies ran while one was open for 0% of the time, Pallas kernels for 0%

profile of v3, /device:TPU:1, one launch (start us, length us, event | category | flops | bytes accessed | tf_op | source)
XLA Modules:
  0.0 105.5 jit_solution(16938754749523728267)
XLA Ops:
  0.6 2.5 %shard_map.58.merged_hbm = bf16[128,4096]{1,0:T(8,128)(2,1)} custom-call(bf16[1,128,4096]{2,1,0:T(8,128)(2,1)} %grad_hbm.1, bf16[1,128,4096]{2,1,0:T(8,128)(2,1)} %error_hbm.1), custom_call_target="tpu_custom_call" | custom-call | tf_op jit(solution)/shard_map/pallas_call | solution.py:66
  3.1 0.0 copy-start.1
  3.1 6.0 %all-to-all-start = ((bf16[8,16,4096]{2,1,0:T(8,128)(2,1)}), bf16[8,16,4096]{2,1,0:T(8,128)(2,1)S(1)}, u32[]{:S(2)}, u32[]{:S(2)}) async-start(bf16[8,16,4096]{2,1,0:T(8,128)(2,1)} %bitcast.3), calls=%async_computation | async-start | bytes 2097152 | tf_op jit(solution)/shard_map/all_to_all | solution.py:289
  9.1 0.0 copy-done.1
  9.2 25.4 %all_gather.15.warm_ref = bf16[64,4096]{1,0:T(8,128)(2,1)S(1)} all-gather(bf16[64,256]{1,0:T(8,128)(2,1)S(1)} %convert_element_type.3), channel_id=1, replica_groups=mesh['yh'=4,'yl'=2,'x'=4,'z'=8,'core'=2] {'z','core'}, dimensions={1}, use_global_device_ids=true | all-gather | bytes 557056 | tf_op jit(solution)/shard_map/all_gather | solution.py:290
  34.6 0.0 all-to-all-done.landed_ref
  34.6 0.7 shard_map.59
  35.3 13.5 %all_to_all.25.landed_ref = bf16[4,16,1280]{2,1,0:T(8,128)(2,1)S(1)} all-to-all(bf16[4,16,1280]{2,1,0:T(8,128)(2,1)S(1)} %shard_map.59), channel_id=1, replica_groups=mesh['yh'=4,'yl'=2,'x'=4,'z'=8,'core'=2] {'yh'}, dimensions={0} | all-to-all | bytes 327680 | tf_op jit(solution)/shard_map/all_to_all | solution.py:292
  48.8 0.5 shard_map.60
  49.3 15.3 %all_to_all.26.landed_ref = f32[16,40,128]{2,1,0:T(8,128)S(1)} all-to-all(f32[16,40,128]{2,1,0:T(8,128)S(1)} %shard_map.60), channel_id=1, replica_groups=mesh['yh'=4,'yl'=2,'x'=4,'z'=8,'core'=2] {'yl','x','core'}, dimensions={0} | all-to-all | bytes 655360 | tf_op jit(solution)/shard_map/all_to_all | solution.py:294
  64.5 0.4 shard_map.61
  64.9 11.0 %all_to_all.27 = f32[8,48,128]{2,1,0:T(8,128)S(1)} all-to-all(f32[8,48,128]{2,1,0:T(8,128)S(1)} %get-tuple-element.7), channel_id=1, replica_groups=mesh['yh'=4,'yl'=2,'x'=4,'z'=8,'core'=2] {'z'}, dimensions={0} | all-to-all | bytes 393216 | tf_op jit(solution)/shard_map/all_to_all | solution.py:300
  75.9 0.0 copy-start
  75.9 4.6 %all-gather = f32[16,48,128]{2,1,0:T(8,128)S(1)} all-gather(f32[8,48,128]{2,1,0:T(8,128)S(1)} %all_to_all.27), channel_id=2, replica_groups=mesh['yh'=4,'yl'=2,'x'=4,'z'=8,'core'=2] {'core'}, dimensions={0}, use_global_device_ids=true | all-gather | bytes 589824 | tf_op jit(solution)/shard_map/all_gather | solution.py:300
  80.6 2.7 %shard_map.62 = (bf16[32,32,128]{2,1,0:T(8,128)(2,1)S(1)}, bf16[128,64]{1,0:T(8,128)(2,1)S(1)}) custom-call(f32[2,8,48,128]{3,2,1,0:T(8,128)S(1)} %bitcast.5, f32[128,64]{1,0:T(8,128)S(1)} %get-tuple-element.8.left_ref), custom_call_target="tpu_custom_call" | custom-call | tf_op jit(solution)/shard_map/pallas_call | solution.py:27
  83.3 15.6 %all_to_all.28 = bf16[32,32,128]{2,1,0:T(8,128)(2,1)S(1)} all-to-all(bf16[32,32,128]{2,1,0:T(8,128)(2,1)S(1)} %get-tuple-element.9), channel_id=1, replica_groups=mesh['yh'=4,'yl'=2,'x'=4,'z'=8,'core'=2] {'yh','yl','x'}, dimensions={0} | all-to-all | bytes 524288 | tf_op jit(solution)/shard_map/all_to_all | solution.py:307
  98.9 4.1 %all-gather.1 = bf16[64,32,128]{2,1,0:T(8,128)(2,1)S(1)} all-gather(bf16[32,32,128]{2,1,0:T(8,128)(2,1)S(1)} %all_to_all.28), channel_id=3, replica_groups=mesh['yh'=4,'yl'=2,'x'=4,'z'=8,'core'=2] {'core'}, dimensions={0}, use_global_device_ids=true | all-gather | bytes 786432 | tf_op jit(solution)/shard_map/all_gather | solution.py:307
  103.0 0.0 copy-done
  103.0 2.5 %shard_map.63 = (bf16[1,128,4096]{2,1,0:T(8,128)(2,1)}, bf16[128,128]{1,0:T(8,128)(2,1)}, f32[64,256]{1,0:T(8,128)}) custom-call(bf16[2,32,32,128]{3,2,1,0:T(8,128)(2,1)S(1)} %bitcast.4, bf16[128,64]{1,0:T(8,128)(2,1)S(1)} %get-tuple-element.10.ortho_ref, bf16[128,4096]{1,0:T(8,128)(2,1)S(1)} %copy-done), custom_call_target="tpu_custom_call" | custom-call | tf_op jit(solution)/shard_map/pallas_call | solution.py:262
  (1 shorter events, 0.0 us)
Async XLA Ops:
  3.1 6.0 %copy-start.1 = (f32[64,256]{1,0:T(8,128)S(1)}, f32[64,256]{1,0:T(8,128)}, u32[]{:S(2)}) copy-start(f32[64,256]{1,0:T(8,128)} %param.5) | copy-start | bytes 196612
  3.1 31.4 %all-to-all-start = ((bf16[8,16,4096]{2,1,0:T(8,128)(2,1)}), bf16[8,16,4096]{2,1,0:T(8,128)(2,1)S(1)}, u32[]{:S(2)}, u32[]{:S(2)}) async-start(bf16[8,16,4096]{2,1,0:T(8,128)(2,1)} %bitcast.3), calls=%async_computation | async-start | bytes 2097152 | tf_op jit(solution)/shard_map/all_to_all | solution.py:289
  75.9 27.0 %copy-start = (bf16[128,4096]{1,0:T(8,128)(2,1)S(1)}, bf16[128,4096]{1,0:T(8,128)(2,1)}, u32[]{:S(2)}) copy-start(bf16[128,4096]{1,0:T(8,128)(2,1)} %shard_map.58.merged_hbm) | copy-start | bytes 3145732

commit v4 on v3

--- a/solution.py
+++ b/solution.py
@@ -10,11 +10,11 @@
 DP = ("yh", "yl", "x")
 FSDP = ("z", "core")
 NEARS = YL * X
-CUTS = 8
+CUTS = 4
 SPANS = 4
 REPLICAS = YH * YL * X
 RANK = 64
-HALF, QUARTER = RANK // 2, RANK // 4
+HALF = RANK // 2
 EXACT = lax.Precision.HIGHEST
 F32, BF16 = jnp.float32, jnp.bfloat16
 VMEM = pl.BlockSpec(memory_space=pltpu.VMEM)
@@ -74,6 +74,10 @@
     )(grad, error)
 
 
+def fold(square):
+    return jnp.concatenate([square[:HALF], square[HALF:]], axis=1)
+
+
 def left_kernel(landed_ref, warm_ref, out_ref):
     _, rows, col_count = landed_ref.shape
     wide = col_count // YH
@@ -118,11 +122,11 @@
     cols = wide // NEARS
     rows = left.shape[0] // 2
     folded_left = jnp.concatenate([left[:rows], left[rows:]], axis=1)
-    for core in range(CORES):
-        for near in range(NEARS):
+    for near in range(NEARS):
+        block = q_terms[:, near * cols : (near + 1) * cols]
+        for core in range(CORES):
             peer = near * CORES + core
-            span = slice(near * cols, (near + 1) * cols)
-            out_ref[peer, :HALF] = q_terms[core * HALF : (core + 1) * HALF, span]
+            out_ref[peer, :HALF] = fold(block[:, core * RANK : (core + 1) * RANK])
             out_ref[peer, HALF:] = folded_left
 
 
@@ -145,24 +149,23 @@
     gram = lax.dot_general(
         both, both, (((0,), (0,)), ((), ())), precision=EXACT, preferred_element_type=F32
     )
-    own = jnp.where(core == 0, gram[:HALF], gram[HALF:])
-    folded = jnp.concatenate([own[:QUARTER], own[QUARTER:]], axis=1)
+    folded = fold(gram)
     for z in range(Z):
         out_ref[z, :HALF] = total
         out_ref[z, HALF:] = folded
 
 
 def factor_kernel(landed_ref, left_ref, q_ref, ortho_ref):
-    sums = landed_ref[:, 0]
+    sums = landed_ref[0]
     for z in range(1, Z):
-        sums = sums + landed_ref[:, z]
+        sums = sums + landed_ref[z]
     lane = lax.broadcasted_iota(jnp.int32, (8, 2 * RANK), 1)
     sub = lax.broadcasted_iota(jnp.int32, (8, 2 * RANK), 0)
     blocks = []
     for b in range(RANK // 8):
-        core, at = divmod(b, 4)
-        raw = sums[core, HALF + 8 * (at % 2) : HALF + 8 * (at % 2) + 8, :]
-        if at >= 2:
+        at = HALF + 8 * (b % 4)
+        raw = sums[at : at + 8]
+        if b >= 4:
             raw = pltpu.roll(raw, RANK, 1)
         unit = (lane == sub + RANK + 8 * b).astype(F32)
         blocks.append(jnp.where(lane < RANK, raw, unit))
@@ -204,12 +207,10 @@
             blocks[t] = blocks[t] - update
     inverse = jnp.concatenate(inverse_rows, axis=0)[:, RANK:]
 
-    q_sum = jnp.concatenate([sums[0, :HALF], sums[1, :HALF]], axis=0)
-    q_mine = jnp.dot(inverse, q_sum, precision=EXACT, preferred_element_type=F32).astype(BF16)
-    core = lax.axis_index("core")
-    q_half = jnp.where(core == 0, q_mine[:HALF], q_mine[HALF:])
+    q_sum = jnp.concatenate([sums[:HALF, :RANK], sums[:HALF, RANK:]], axis=0)
+    q_mine = fold(jnp.dot(inverse, q_sum, precision=EXACT, preferred_element_type=F32)).astype(BF16)
     for peer in range(q_ref.shape[0]):
-        q_ref[peer] = q_half
+        q_ref[peer] = q_mine
     ortho_ref[...] = lax.dot_general(
         left_ref[...],
         inverse,
@@ -220,38 +221,35 @@
 
 
 def rebuild_kernel(
-    q_ref, ortho_ref, merged_hbm, error_hbm, own_ref, q_next_ref, q_all, merged, error, in_sems, out_sems
+    q_ref, ortho_ref, merged, error_hbm, own_ref, q_next_ref, q_all, error, out_sems
 ):
     cols = q_ref.shape[3]
     col_count = merged.shape[1]
     wide = col_count // SPANS
-    ins, outs = [], []
+    outs = []
     for i in range(SPANS):
         span = pl.ds(i * wide, wide)
-        ins.append(pltpu.make_async_copy(merged_hbm.at[:, span], merged.at[:, span], in_sems.at[i]))
         outs.append(
             pltpu.make_async_copy(error.at[:, span], error_hbm.at[0, :, span], out_sems.at[i])
         )
-        ins[i].start()
     for d in range(REPLICAS):
-        q_all[:HALF, d * cols : (d + 1) * cols] = q_ref[0, d]
-        q_all[HALF:, d * cols : (d + 1) * cols] = q_ref[1, d]
+        first, second = q_ref[0, d], q_ref[1, d]
+        span = slice(d * cols, (d + 1) * cols)
+        q_all[:HALF, span] = jnp.concatenate([first[:, :RANK], second[:, :RANK]], axis=1)
+        q_all[HALF:, span] = jnp.concatenate([first[:, RANK:], second[:, RANK:]], axis=1)
     ortho = ortho_ref[...]
     for i in range(SPANS):
         span = slice(i * wide, (i + 1) * wide)
         approx = jnp.dot(ortho, q_all[:, span], preferred_element_type=F32)
-        ins[i].wait()
         error[:, span] = (merged[:, span].astype(F32) - approx).astype(BF16)
         outs[i].start()
 
     own = (lax.axis_index("yh") * YL + lax.axis_index("yl")) * X + lax.axis_index("x")
-    right = jnp.concatenate([q_ref[0, own], q_ref[1, own]], axis=0)
+    right = q_all[:, pl.ds(pl.multiple_of(own * cols, cols), cols)]
     own_ref[...] = jnp.dot(ortho, right, preferred_element_type=F32).astype(BF16)
-    count = q_next_ref.shape[1] // cols
-    first = (lax.axis_index("z") * CORES + lax.axis_index("core")) * count
-    for i in range(count):
-        q_next_ref[:HALF, i * cols : (i + 1) * cols] = q_ref[0, first + i].astype(F32)
-        q_next_ref[HALF:, i * cols : (i + 1) * cols] = q_ref[1, first + i].astype(F32)
+    shard = q_next_ref.shape[1]
+    first = (lax.axis_index("z") * CORES + lax.axis_index("core")) * shard
+    q_next_ref[...] = q_all[:, pl.ds(pl.multiple_of(first, shard), shard)].astype(F32)
     for i in range(SPANS):
         outs[i].wait()
 
@@ -266,13 +264,11 @@
             shape(BF16, rows, cols),
             shape(F32, RANK, shard),
         ),
-        in_specs=[VMEM, VMEM, ANY],
+        in_specs=[VMEM, VMEM, VMEM],
         out_specs=[ANY, VMEM, VMEM],
         scratch_shapes=[
             pltpu.VMEM((RANK, col_count), BF16),
             pltpu.VMEM((rows, col_count), BF16),
-            pltpu.VMEM((rows, col_count), BF16),
-            pltpu.SemaphoreType.DMA((SPANS,)),
             pltpu.SemaphoreType.DMA((SPANS,)),
         ],
         compiler_params=pltpu.CompilerParams(vmem_limit_bytes=LIMIT),
@@ -294,10 +290,10 @@
     landed = lax.all_to_all(to_near, NEAR + ("core",), 0, 0)
     terms, left = call(
         spread_kernel,
-        (shape(F32, Z, HALF + QUARTER, cols), shape(F32, rows, RANK)),
+        (shape(F32, Z, 2 * HALF, cols), shape(F32, rows, RANK)),
         landed,
     )
-    terms = lax.all_gather(lax.all_to_all(terms, "z", 0, 0), "core")
+    terms = lax.all_to_all(terms, "z", 0, 0)
     q_copies, ortho = call(
         factor_kernel,
         (shape(BF16, REPLICAS, HALF, cols), shape(BF16, rows, RANK)),

time: 106 us -> 104 us (0.981)
    all_gather x1 -> x0, blocking collectives: 4.64 us -> none  [on_device(): terms = lax.all_gather(lax.all_to_all(terms, 'z', 0, 0), 'core')]
    all_to_all x1, blocking collectives: 15.6 us -> 18 us  [on_device(): q_all = lax.all_gather(lax.all_to_all(q_copies, DP, 0, 0), 'core')]
    all_to_all x1, blocking collectives: 11 us -> 12.6 us  [on_device(): terms = lax.all_to_all(terms, 'z', 0, 0)]
where the time goes in v4:
time: 104 us
  blocking collectives  88.6 us (85%)
  Pallas kernels  8.69 us (8%)
  starting transfers between devices  6.01 us (6%)
    all_gather x1, blocking collectives, on_device(): warm = lax.all_gather(q_warm.astype(BF16), FSDP, axis=1, tiled=True)  25.4 us
    all_to_all x1, blocking collectives, on_device(): q_all = lax.all_gather(lax.all_to_all(q_copies, DP, 0, 0), 'core')  18 us
    all_to_all x1, blocking collectives, on_device(): landed = lax.all_to_all(to_near, NEAR + ('core',), 0, 0)  15.2 us
    all_to_all x1, blocking collectives, on_device(): landed = lax.all_to_all(to_far, 'yh', 0, 0)  13.5 us
    all_to_all x1, blocking collectives, on_device(): terms = lax.all_to_all(terms, 'z', 0, 0)  12.6 us
    all_to_all x1, starting transfers between devices, on_device(): landed = lax.all_to_all(merged.reshape(NEARS, part, col_count), NEAR, 0, 0)  6.01 us
    pallas_call x4, Pallas kernels, call(): pl.pallas_call(kernel, out_shape=out, in_specs=[VMEM] * len(operands), ou...  4.36 us
    all_gather x1, blocking collectives, on_device(): q_all = lax.all_gather(lax.all_to_all(q_copies, DP, 0, 0), 'core')  4.02 us
  transfers between devices with their start and end apart: 1, of which 0 were waited for; matrix products, arithmetic and copies ran while one was open for 0% of the time, Pallas kernels for 0%

profile of v4, /device:TPU:1, one launch (start us, length us, event | category | flops | bytes accessed | tf_op | source)
XLA Modules:
  0.0 104.0 jit_solution(17817100757611527722)
XLA Ops:
  0.6 2.4 %shard_map.58.merged = bf16[128,4096]{1,0:T(8,128)(2,1)} custom-call(bf16[1,128,4096]{2,1,0:T(8,128)(2,1)} %grad_hbm.1, bf16[1,128,4096]{2,1,0:T(8,128)(2,1)} %error_hbm.1), custom_call_target="tpu_custom_call" | custom-call | tf_op jit(solution)/shard_map/pallas_call | solution.py:66
  3.0 0.0 copy-start.1
  3.0 6.0 %all-to-all-start = ((bf16[8,16,4096]{2,1,0:T(8,128)(2,1)}), bf16[8,16,4096]{2,1,0:T(8,128)(2,1)S(1)}, u32[]{:S(2)}, u32[]{:S(2)}) async-start(bf16[8,16,4096]{2,1,0:T(8,128)(2,1)} %bitcast.2), calls=%async_computation | async-start | bytes 2097152 | tf_op jit(solution)/shard_map/all_to_all | solution.py:285
  9.0 0.0 copy-done.1
  9.0 25.4 %all_gather.9.warm_ref = bf16[64,4096]{1,0:T(8,128)(2,1)S(1)} all-gather(bf16[64,256]{1,0:T(8,128)(2,1)S(1)} %convert_element_type.3), channel_id=1, replica_groups=mesh['yh'=4,'yl'=2,'x'=4,'z'=8,'core'=2] {'z','core'}, dimensions={1}, use_global_device_ids=true | all-gather | bytes 557056 | tf_op jit(solution)/shard_map/all_gather | solution.py:286
  34.4 0.0 all-to-all-done.landed_ref
  34.4 0.7 shard_map.59
  35.1 13.5 %all_to_all.25.landed_ref = bf16[4,16,1280]{2,1,0:T(8,128)(2,1)S(1)} all-to-all(bf16[4,16,1280]{2,1,0:T(8,128)(2,1)S(1)} %shard_map.59), channel_id=1, replica_groups=mesh['yh'=4,'yl'=2,'x'=4,'z'=8,'core'=2] {'yh'}, dimensions={0} | all-to-all | bytes 327680 | tf_op jit(solution)/shard_map/all_to_all | solution.py:288
  48.6 0.6 shard_map.60
  49.2 15.2 %all_to_all.26.landed_ref = f32[16,40,128]{2,1,0:T(8,128)S(1)} all-to-all(f32[16,40,128]{2,1,0:T(8,128)S(1)} %shard_map.60), channel_id=1, replica_groups=mesh['yh'=4,'yl'=2,'x'=4,'z'=8,'core'=2] {'yl','x','core'}, dimensions={0} | all-to-all | bytes 655360 | tf_op jit(solution)/shard_map/all_to_all | solution.py:290
  64.4 0.4 shard_map.61
  64.8 0.0 copy-start
  64.8 12.6 %all_to_all.27.landed_ref = f32[8,64,128]{2,1,0:T(8,128)S(1)} all-to-all(f32[8,64,128]{2,1,0:T(8,128)S(1)} %get-tuple-element.7), channel_id=1, replica_groups=mesh['yh'=4,'yl'=2,'x'=4,'z'=8,'core'=2] {'z'}, dimensions={0} | all-to-all | bytes 524288 | tf_op jit(solution)/shard_map/all_to_all | solution.py:296
  77.4 2.7 %shard_map.62 = (bf16[32,32,128]{2,1,0:T(8,128)(2,1)S(1)}, bf16[128,64]{1,0:T(8,128)(2,1)S(1)}) custom-call(f32[8,64,128]{2,1,0:T(8,128)S(1)} %all_to_all.27.landed_ref, f32[128,64]{1,0:T(8,128)S(1)} %get-tuple-element.8.left_ref), custom_call_target="tpu_custom_call" | custom-call | tf_op jit(solution)/shard_map/pallas_call | solution.py:27
  80.1 18.0 %all_to_all.28 = bf16[32,32,128]{2,1,0:T(8,128)(2,1)S(1)} all-to-all(bf16[32,32,128]{2,1,0:T(8,128)(2,1)S(1)} %get-tuple-element.9), channel_id=1, replica_groups=mesh['yh'=4,'yl'=2,'x'=4,'z'=8,'core'=2] {'yh','yl','x'}, dimensions={0} | all-to-all | bytes 524288 | tf_op jit(solution)/shard_map/all_to_all | solution.py:303
  98.1 4.0 %all-gather = bf16[64,32,128]{2,1,0:T(8,128)(2,1)S(1)} all-gather(bf16[32,32,128]{2,1,0:T(8,128)(2,1)S(1)} %all_to_all.28), channel_id=2, replica_groups=mesh['yh'=4,'yl'=2,'x'=4,'z'=8,'core'=2] {'core'}, dimensions={0}, use_global_device_ids=true | all-gather | bytes 786432 | tf_op jit(solution)/shard_map/all_gather | solution.py:303
  102.1 0.0 copy-done
  102.1 2.0 %shard_map.63 = (bf16[1,128,4096]{2,1,0:T(8,128)(2,1)}, bf16[128,128]{1,0:T(8,128)(2,1)}, f32[64,256]{1,0:T(8,128)}) custom-call(bf16[2,32,32,128]{3,2,1,0:T(8,128)(2,1)S(1)} %bitcast.3, bf16[128,64]{1,0:T(8,128)(2,1)S(1)} %get-tuple-element.10.ortho_ref, bf16[128,4096]{1,0:T(8,128)(2,1)S(1)} %copy-done), custom_call_target="tpu_custom_call" | custom-call | tf_op jit(solution)/shard_map/pallas_call | solution.py:260
  (1 shorter events, 0.0 us)
Async XLA Ops:
  3.0 6.0 %copy-start.1 = (f32[64,256]{1,0:T(8,128)S(1)}, f32[64,256]{1,0:T(8,128)}, u32[]{:S(2)}) copy-start(f32[64,256]{1,0:T(8,128)} %param.5) | copy-start | bytes 196612
  3.0 31.4 %all-to-all-start = ((bf16[8,16,4096]{2,1,0:T(8,128)(2,1)}), bf16[8,16,4096]{2,1,0:T(8,128)(2,1)S(1)}, u32[]{:S(2)}, u32[]{:S(2)}) async-start(bf16[8,16,4096]{2,1,0:T(8,128)(2,1)} %bitcast.2), calls=%async_computation | async-start | bytes 2097152 | tf_op jit(solution)/shard_map/all_to_all | solution.py:285
  64.8 37.3 %copy-start = (bf16[128,4096]{1,0:T(8,128)(2,1)S(1)}, bf16[128,4096]{1,0:T(8,128)(2,1)}, u32[]{:S(2)}) copy-start(bf16[128,4096]{1,0:T(8,128)(2,1)} %shard_map.58.merged) | copy-start | bytes 3145732

commit v5 on v4

--- a/solution.py
+++ b/solution.py
@@ -79,80 +79,66 @@
 
 
 def left_kernel(landed_ref, warm_ref, out_ref):
-    _, rows, col_count = landed_ref.shape
-    wide = col_count // YH
-    stacked = landed_ref[...].reshape(NEARS * rows, col_count)
+    near, rows, col_count = landed_ref.shape
+    stacked = landed_ref[...].reshape(near * rows, col_count)
     every = lax.dot_general(
         stacked, warm_ref[...], (((1,), (1,)), ((), ())), preferred_element_type=F32
     )
     left = every[:rows]
-    for peer in range(1, NEARS):
-        left = left + every[peer * rows : (peer + 1) * rows]
+    for n in range(1, near):
+        left = left + every[n * rows : (n + 1) * rows]
     high = left.astype(BF16)
-    rest = left - high.astype(F32)
-    middle = rest.astype(BF16)
-    low = (rest - middle.astype(F32)).astype(BF16)
-    first = jnp.concatenate([high, middle], axis=1)
-    second = jnp.concatenate([low, jnp.zeros_like(low)], axis=1)
-    for y in range(YH):
-        span = pl.ds(y * wide, wide)
+    left = jnp.concatenate([high, (left - high.astype(F32)).astype(BF16)], axis=1)
+    cols = col_count // REPLICAS
+    for d in range(REPLICAS):
+        span = pl.ds(d * cols, cols)
         total = landed_ref[0, :, span].astype(F32)
-        for peer in range(1, NEARS):
-            total = total + landed_ref[peer, :, span].astype(F32)
-        out_ref[y, :, :wide] = total.astype(BF16)
-        out_ref[y, :, wide : wide + 2 * RANK] = first
-        out_ref[y, :, wide + 2 * RANK :] = second
-
-
-def terms_kernel(landed_ref, out_ref):
-    total = landed_ref[0].astype(F32)
+        for n in range(1, near):
+            total = total + landed_ref[n, :, span].astype(F32)
+        out_ref[d, :rows] = total.astype(BF16)
+        out_ref[d, rows:] = left
+
+
+def mean_kernel(landed_ref, out_ref):
+    rows = landed_ref.shape[1] // 2
+    total = landed_ref[:NEARS].astype(F32)
     for y in range(1, YH):
-        total = total + landed_ref[y].astype(F32)
-    wide = total.shape[1] - 4 * RANK
+        total = total + landed_ref[y * NEARS : (y + 1) * NEARS].astype(F32)
     total = total * (1.0 / REPLICAS)
-    mean = total[:, :wide]
-    left = (
-        total[:, wide : wide + RANK]
-        + total[:, wide + RANK : wide + 2 * RANK]
-        + total[:, wide + 2 * RANK : wide + 3 * RANK]
-    )
-    q_terms = lax.dot_general(
-        left, mean, (((0,), (0,)), ((), ())), precision=EXACT, preferred_element_type=F32
-    )
-    cols = wide // NEARS
-    rows = left.shape[0] // 2
-    folded_left = jnp.concatenate([left[:rows], left[rows:]], axis=1)
-    for near in range(NEARS):
-        block = q_terms[:, near * cols : (near + 1) * cols]
-        for core in range(CORES):
-            peer = near * CORES + core
-            out_ref[peer, :HALF] = fold(block[:, core * RANK : (core + 1) * RANK])
-            out_ref[peer, HALF:] = folded_left
-
-
-def spread_kernel(landed_ref, out_ref, left_ref):
+    out_ref[:, :rows] = total[:, :rows]
+    left = total[:, rows:, :RANK] + total[:, rows:, RANK:]
+    half = rows // 2
+    out_ref[:, rows:] = jnp.concatenate([left[:, :half], left[:, half:]], axis=2)
+
+
+def terms_kernel(means_ref, out_ref, left_ref):
+    near, rows = means_ref.shape[1], left_ref.shape[0] // NEARS
     core = lax.axis_index("core")
-    total = landed_ref[0, :HALF]
-    for peer in range(1, NEARS * CORES):
-        total = total + landed_ref[peer, :HALF]
 
     def left_of(which):
         pieces = []
-        for near in range(NEARS):
-            piece = landed_ref[near * CORES + which, HALF:]
+        for n in range(near):
+            piece = means_ref[which, n, rows:]
             pieces += [piece[:, :RANK], piece[:, RANK:]]
         return jnp.concatenate(pieces, axis=0)
 
+    def mean_of(which):
+        return jnp.concatenate([means_ref[which, n, :rows] for n in range(near)], axis=0)
+
     mine, other = left_of(core), left_of(1 - core)
     left_ref[...] = mine
-    both = jnp.concatenate([mine, other], axis=0)
-    gram = lax.dot_general(
-        both, both, (((0,), (0,)), ((), ())), precision=EXACT, preferred_element_type=F32
-    )
-    folded = fold(gram)
+    left = jnp.concatenate([mine, other], axis=0)
+    mean = jnp.concatenate([mean_of(core), mean_of(1 - core)], axis=0)
+    mean = jnp.where(core == 0, mean[:, :RANK], mean[:, RANK:])
+    terms = lax.dot_general(
+        left,
+        jnp.concatenate([left, mean], axis=1),
+        (((0,), (0,)), ((), ())),
+        precision=EXACT,
+        preferred_element_type=F32,
+    )
     for z in range(Z):
-        out_ref[z, :HALF] = total
-        out_ref[z, HALF:] = folded
+        out_ref[z] = terms
 
 
 def factor_kernel(landed_ref, left_ref, q_ref, ortho_ref):
@@ -163,12 +149,8 @@
     sub = lax.broadcasted_iota(jnp.int32, (8, 2 * RANK), 0)
     blocks = []
     for b in range(RANK // 8):
-        at = HALF + 8 * (b % 4)
-        raw = sums[at : at + 8]
-        if b >= 4:
-            raw = pltpu.roll(raw, RANK, 1)
         unit = (lane == sub + RANK + 8 * b).astype(F32)
-        blocks.append(jnp.where(lane < RANK, raw, unit))
+        blocks.append(jnp.where(lane < RANK, sums[8 * b : 8 * b + 8], unit))
 
     def lane_copy(value, column):
         return jnp.broadcast_to(value[:, column : column + 1], value.shape)
@@ -183,31 +165,36 @@
         later = [
             [lane_copy(blocks[t], 8 * b + j) for j in range(8)] for t in range(b + 1, RANK // 8)
         ]
-        scales = jnp.zeros_like(here)
+        entry = [[row_copy(columns[k], i) for k in range(i + 1)] for i in range(8)]
+        row = [row_copy(here, i) for i in range(8)]
+        recip = [None] * 8
+        factor = [[None] * 8 for _ in range(8)]
         for j in range(8):
-            pivot = row_copy(columns[j], j)
-            recip = 1.0 / pivot
-            scales = jnp.where(sub == j, recip, scales)
-            factor = jnp.where(sub > j, columns[j] * recip, 0.0)
-            here = here - factor * row_copy(here, j)
-            for other in range(j + 1, 8):
-                columns[other] = columns[other] - factor * row_copy(columns[other], j)
-        inverse_rows.append(here * jnp.sqrt(scales))
+            recip[j] = 1.0 / entry[j][j]
+            for i in range(j + 1, 8):
+                factor[i][j] = entry[i][j] * recip[j]
+            for i in range(j + 1, 8):
+                for k in range(j + 1, i + 1):
+                    entry[i][k] = entry[i][k] - factor[i][j] * entry[k][j]
+                row[i] = row[i] - factor[i][j] * row[j]
+        done = row[0] * jnp.sqrt(recip[0])
+        for i in range(1, 8):
+            done = jnp.where(sub == i, row[i] * jnp.sqrt(recip[i]), done)
+        inverse_rows.append(done)
         if b + 1 == RANK // 8:
             break
-        solved = here * scales
-        uppers = [columns[j] * scales for j in range(8)]
-        for j in range(7, 0, -1):
-            factor = jnp.where(sub < j, uppers[j], 0.0)
-            solved = solved - factor * row_copy(solved, j)
+        solved = [row[i] * recip[i] for i in range(8)]
+        for i in range(7, 0, -1):
+            for j in range(i):
+                solved[j] = solved[j] - factor[i][j] * solved[i]
         for t in range(b + 1, RANK // 8):
-            update = later[t - b - 1][0] * row_copy(solved, 0)
+            update = later[t - b - 1][0] * solved[0]
             for j in range(1, 8):
-                update = update + later[t - b - 1][j] * row_copy(solved, j)
+                update = update + later[t - b - 1][j] * solved[j]
             blocks[t] = blocks[t] - update
     inverse = jnp.concatenate(inverse_rows, axis=0)[:, RANK:]
 
-    q_sum = jnp.concatenate([sums[:HALF, :RANK], sums[:HALF, RANK:]], axis=0)
+    q_sum = sums[:, RANK:]
     q_mine = fold(jnp.dot(inverse, q_sum, precision=EXACT, preferred_element_type=F32)).astype(BF16)
     for peer in range(q_ref.shape[0]):
         q_ref[peer] = q_mine
@@ -232,14 +219,14 @@
         outs.append(
             pltpu.make_async_copy(error.at[:, span], error_hbm.at[0, :, span], out_sems.at[i])
         )
-    for d in range(REPLICAS):
-        first, second = q_ref[0, d], q_ref[1, d]
-        span = slice(d * cols, (d + 1) * cols)
-        q_all[:HALF, span] = jnp.concatenate([first[:, :RANK], second[:, :RANK]], axis=1)
-        q_all[HALF:, span] = jnp.concatenate([first[:, RANK:], second[:, RANK:]], axis=1)
     ortho = ortho_ref[...]
     for i in range(SPANS):
         span = slice(i * wide, (i + 1) * wide)
+        for d in range(i * wide // cols, (i + 1) * wide // cols):
+            first, second = q_ref[0, d], q_ref[1, d]
+            block = slice(d * cols, (d + 1) * cols)
+            q_all[:HALF, block] = jnp.concatenate([first[:, :RANK], second[:, :RANK]], axis=1)
+            q_all[HALF:, block] = jnp.concatenate([first[:, RANK:], second[:, RANK:]], axis=1)
         approx = jnp.dot(ortho, q_all[:, span], preferred_element_type=F32)
         error[:, span] = (merged[:, span].astype(F32) - approx).astype(BF16)
         outs[i].start()
@@ -278,20 +265,18 @@
 def on_device(grad, error, q_warm):
     rows, col_count = grad.shape[1:]
     cols = col_count // REPLICAS
-    wide = col_count // YH
     part = rows // NEARS
     merged = merge(grad, error)
 
     landed = lax.all_to_all(merged.reshape(NEARS, part, col_count), NEAR, 0, 0)
     warm = lax.all_gather(q_warm.astype(BF16), FSDP, axis=1, tiled=True)
-    to_far = call(left_kernel, shape(BF16, YH, part, wide + 4 * RANK), landed, warm)
-    landed = lax.all_to_all(to_far, "yh", 0, 0)
-    to_near = call(terms_kernel, shape(F32, NEARS * CORES, HALF + part // 2, cols), landed)
-    landed = lax.all_to_all(to_near, NEAR + ("core",), 0, 0)
+    shares = call(left_kernel, shape(BF16, REPLICAS, 2 * part, cols), landed, warm)
+    shares = lax.all_to_all(shares, DP, 0, 0)
+    means = call(mean_kernel, shape(F32, NEARS, part + part // 2, cols), shares)
     terms, left = call(
-        spread_kernel,
-        (shape(F32, Z, 2 * HALF, cols), shape(F32, rows, RANK)),
-        landed,
+        terms_kernel,
+        (shape(F32, Z, RANK, 2 * RANK), shape(F32, rows, RANK)),
+        lax.all_gather(means, "core"),
     )
     terms = lax.all_to_all(terms, "z", 0, 0)
     q_copies, ortho = call(

time: 104 us -> 98.6 us (0.948)
  blocking collectives: 88.6 us -> 83.5 us
    all_to_all x2 -> x1, blocking collectives: 28.7 us -> 20.9 us  [on_device(): shares = lax.all_to_all(shares, DP, 0, 0)]
    all_gather x0 -> x1, blocking collectives: none -> 3.73 us  [on_device(): lax.all_gather(means, 'core')]
    all_to_all x1, blocking collectives: 18 us -> 14.8 us  [on_device(): q_all = lax.all_gather(lax.all_to_all(q_copies, DP, 0, 0), 'core')]
    all_to_all x1, blocking collectives: 12.6 us -> 14.8 us  [on_device(): terms = lax.all_to_all(terms, 'z', 0, 0)]
where the time goes in v5:
time: 98.6 us; the launch traced here: 98.3 us
  blocking collectives  83.5 us (85%)
  Pallas kernels  8.02 us (8%)
  starting transfers between devices  6.01 us (6%)
    all_gather x1, blocking collectives, on_device(): warm = lax.all_gather(q_warm.astype(BF16), FSDP, axis=1, tiled=True)  25.4 us
    all_to_all x1, blocking collectives, on_device(): shares = lax.all_to_all(shares, DP, 0, 0)  20.9 us
    all_to_all x1, blocking collectives, on_device(): terms = lax.all_to_all(terms, 'z', 0, 0)  14.8 us
    all_to_all x1, blocking collectives, on_device(): q_all = lax.all_gather(lax.all_to_all(q_copies, DP, 0, 0), 'core')  14.8 us
    all_to_all x1, starting transfers between devices, on_device(): landed = lax.all_to_all(merged.reshape(NEARS, part, col_count), NEAR, 0, 0)  6.01 us
    all_gather x1, blocking collectives, on_device(): q_all = lax.all_gather(lax.all_to_all(q_copies, DP, 0, 0), 'core')  3.95 us
    all_gather x1, blocking collectives, on_device(): lax.all_gather(means, 'core')  3.73 us
    pallas_call x4, Pallas kernels, call(): pl.pallas_call(kernel, out_shape=out, in_specs=[VMEM] * len(operands), ou...  3.69 us
  transfers between devices with their start and end apart: 1, of which 0 were waited for; matrix products, arithmetic and copies ran while one was open for 0% of the time, Pallas kernels for 0%

profile of v5, /device:TPU:1, one launch (start us, length us, event | category | flops | bytes accessed | tf_op | source)
XLA Modules:
  0.0 98.3 jit_solution(16296150285456262535)
XLA Ops:
  0.6 2.4 %shard_map.58.merged = bf16[128,4096]{1,0:T(8,128)(2,1)} custom-call(bf16[1,128,4096]{2,1,0:T(8,128)(2,1)} %grad_hbm.1, bf16[1,128,4096]{2,1,0:T(8,128)(2,1)} %error_hbm.1), custom_call_target="tpu_custom_call" | custom-call | tf_op jit(solution)/shard_map/pallas_call | solution.py:66
  3.0 0.0 copy-start.1
  3.0 6.0 %all-to-all-start = ((bf16[8,16,4096]{2,1,0:T(8,128)(2,1)}), bf16[8,16,4096]{2,1,0:T(8,128)(2,1)S(1)}, u32[]{:S(2)}, u32[]{:S(2)}) async-start(bf16[8,16,4096]{2,1,0:T(8,128)(2,1)} %bitcast.3), calls=%async_computation | async-start | bytes 2097152 | tf_op jit(solution)/shard_map/all_to_all | solution.py:271
  9.0 0.0 copy-done.1
  9.0 25.4 %all_gather.15.warm_ref = bf16[64,4096]{1,0:T(8,128)(2,1)S(1)} all-gather(bf16[64,256]{1,0:T(8,128)(2,1)S(1)} %convert_element_type.3), channel_id=1, replica_groups=mesh['yh'=4,'yl'=2,'x'=4,'z'=8,'core'=2] {'z','core'}, dimensions={1}, use_global_device_ids=true | all-gather | bytes 557056 | tf_op jit(solution)/shard_map/all_gather | solution.py:272
  34.4 0.0 all-to-all-done.landed_ref
  34.4 0.7 shard_map.59
  35.1 20.9 %all_to_all.20.landed_ref = bf16[32,32,128]{2,1,0:T(8,128)(2,1)S(1)} all-to-all(bf16[32,32,128]{2,1,0:T(8,128)(2,1)S(1)} %shard_map.59), channel_id=1, replica_groups=mesh['yh'=4,'yl'=2,'x'=4,'z'=8,'core'=2] {'yh','yl','x'}, dimensions={0} | all-to-all | bytes 524288 | tf_op jit(solution)/shard_map/all_to_all | solution.py:274
  56.0 0.2 shard_map.60
  56.2 3.7 %all-gather = f32[16,24,128]{2,1,0:T(8,128)S(1)} all-gather(f32[8,24,128]{2,1,0:T(8,128)S(1)} %shard_map.60), channel_id=2, replica_groups=mesh['yh'=4,'yl'=2,'x'=4,'z'=8,'core'=2] {'core'}, dimensions={0}, use_global_device_ids=true | all-gather | bytes 294912 | tf_op jit(solution)/shard_map/all_gather | solution.py:279
  59.9 0.4 shard_map.61
  60.3 0.0 copy-start
  60.3 14.8 %all_to_all.21.landed_ref = f32[8,64,128]{2,1,0:T(8,128)S(1)} all-to-all(f32[8,64,128]{2,1,0:T(8,128)S(1)} %get-tuple-element.7), channel_id=1, replica_groups=mesh['yh'=4,'yl'=2,'x'=4,'z'=8,'core'=2] {'z'}, dimensions={0} | all-to-all | bytes 524288 | tf_op jit(solution)/shard_map/all_to_all | solution.py:281
  75.1 2.4 %shard_map.62 = (bf16[32,32,128]{2,1,0:T(8,128)(2,1)S(1)}, bf16[128,64]{1,0:T(8,128)(2,1)S(1)}) custom-call(f32[8,64,128]{2,1,0:T(8,128)S(1)} %all_to_all.21.landed_ref, f32[128,64]{1,0:T(8,128)S(1)} %get-tuple-element.8.left_ref), custom_call_target="tpu_custom_call" | custom-call | tf_op jit(solution)/shard_map/pallas_call | solution.py:27
  77.6 14.8 %all_to_all.22 = bf16[32,32,128]{2,1,0:T(8,128)(2,1)S(1)} all-to-all(bf16[32,32,128]{2,1,0:T(8,128)(2,1)S(1)} %get-tuple-element.9), channel_id=1, replica_groups=mesh['yh'=4,'yl'=2,'x'=4,'z'=8,'core'=2] {'yh','yl','x'}, dimensions={0} | all-to-all | bytes 524288 | tf_op jit(solution)/shard_map/all_to_all | solution.py:288
  92.4 3.9 %all-gather.1 = bf16[64,32,128]{2,1,0:T(8,128)(2,1)S(1)} all-gather(bf16[32,32,128]{2,1,0:T(8,128)(2,1)S(1)} %all_to_all.22), channel_id=3, replica_groups=mesh['yh'=4,'yl'=2,'x'=4,'z'=8,'core'=2] {'core'}, dimensions={0}, use_global_device_ids=true | all-gather | bytes 786432 | tf_op jit(solution)/shard_map/all_gather | solution.py:288
  96.3 0.0 copy-done
  96.3 2.0 %shard_map.63 = (bf16[1,128,4096]{2,1,0:T(8,128)(2,1)}, bf16[128,128]{1,0:T(8,128)(2,1)}, f32[64,256]{1,0:T(8,128)}) custom-call(bf16[2,32,32,128]{3,2,1,0:T(8,128)(2,1)S(1)} %bitcast.4, bf16[128,64]{1,0:T(8,128)(2,1)S(1)} %get-tuple-element.10.ortho_ref, bf16[128,4096]{1,0:T(8,128)(2,1)S(1)} %copy-done), custom_call_target="tpu_custom_call" | custom-call | tf_op jit(solution)/shard_map/pallas_call | solution.py:247
  (1 shorter events, 0.0 us)
Async XLA Ops:
  3.0 6.0 %copy-start.1 = (f32[64,256]{1,0:T(8,128)S(1)}, f32[64,256]{1,0:T(8,128)}, u32[]{:S(2)}) copy-start(f32[64,256]{1,0:T(8,128)} %param.5) | copy-start | bytes 196612
  3.0 31.4 %all-to-all-start = ((bf16[8,16,4096]{2,1,0:T(8,128)(2,1)}), bf16[8,16,4096]{2,1,0:T(8,128)(2,1)S(1)}, u32[]{:S(2)}, u32[]{:S(2)}) async-start(bf16[8,16,4096]{2,1,0:T(8,128)(2,1)} %bitcast.3), calls=%async_computation | async-start | bytes 2097152 | tf_op jit(solution)/shard_map/all_to_all | solution.py:271
  60.3 36.0 %copy-start = (bf16[128,4096]{1,0:T(8,128)(2,1)S(1)}, bf16[128,4096]{1,0:T(8,128)(2,1)}, u32[]{:S(2)}) copy-start(bf16[128,4096]{1,0:T(8,128)(2,1)} %shard_map.58.merged) | copy-start | bytes 3145732

commit v6 on v5

--- a/solution.py
+++ b/solution.py
@@ -22,13 +22,14 @@
 LIMIT = 32 * 1024 * 1024
 
 
-def call(kernel, out, *operands):
+def call(kernel, out, *operands, scratch=()):
     many = isinstance(out, (list, tuple))
     return pl.pallas_call(
         kernel,
         out_shape=out,
         in_specs=[VMEM] * len(operands),
         out_specs=[VMEM] * len(out) if many else VMEM,
+        scratch_shapes=list(scratch),
         compiler_params=pltpu.CompilerParams(vmem_limit_bytes=LIMIT),
     )(*operands)
 
@@ -141,7 +142,7 @@
         out_ref[z] = terms
 
 
-def factor_kernel(landed_ref, left_ref, q_ref, ortho_ref):
+def factor_kernel(landed_ref, left_ref, q_ref, ortho_ref, held):
     sums = landed_ref[0]
     for z in range(1, Z):
         sums = sums + landed_ref[z]
@@ -155,8 +156,8 @@
     def lane_copy(value, column):
         return jnp.broadcast_to(value[:, column : column + 1], value.shape)
 
-    def row_copy(value, row):
-        return jnp.broadcast_to(value[row : row + 1], value.shape)
+    def row_copy(slot, row):
+        return jnp.broadcast_to(held[slot, row : row + 1, :], (8, 2 * RANK))
 
     inverse_rows = []
     for b in range(RANK // 8):
@@ -165,8 +166,12 @@
         later = [
             [lane_copy(blocks[t], 8 * b + j) for j in range(8)] for t in range(b + 1, RANK // 8)
         ]
-        entry = [[row_copy(columns[k], i) for k in range(i + 1)] for i in range(8)]
-        row = [row_copy(here, i) for i in range(8)]
+        base = 9 * (b % 2)
+        held[base + 8] = here
+        for k in range(8):
+            held[base + k] = columns[k]
+        entry = [[row_copy(base + k, i) for k in range(i + 1)] for i in range(8)]
+        row = [row_copy(base + 8, i) for i in range(8)]
         recip = [None] * 8
         factor = [[None] * 8 for _ in range(8)]
         for j in range(8):
@@ -195,7 +200,13 @@
     inverse = jnp.concatenate(inverse_rows, axis=0)[:, RANK:]
 
     q_sum = sums[:, RANK:]
-    q_mine = fold(jnp.dot(inverse, q_sum, precision=EXACT, preferred_element_type=F32)).astype(BF16)
+    q_mine = jnp.dot(inverse, q_sum, precision=EXACT, preferred_element_type=F32).astype(BF16)
+    upper, lower = q_mine[:HALF], q_mine[HALF:]
+    q_mine = jnp.where(
+        lax.axis_index("core") == 0,
+        jnp.concatenate([upper, lower], axis=1),
+        jnp.concatenate([lower, upper], axis=1),
+    )
     for peer in range(q_ref.shape[0]):
         q_ref[peer] = q_mine
     ortho_ref[...] = lax.dot_general(
@@ -220,13 +231,15 @@
             pltpu.make_async_copy(error.at[:, span], error_hbm.at[0, :, span], out_sems.at[i])
         )
     ortho = ortho_ref[...]
+    lane = lax.broadcasted_iota(jnp.int32, (HALF, cols), 1)
     for i in range(SPANS):
         span = slice(i * wide, (i + 1) * wide)
         for d in range(i * wide // cols, (i + 1) * wide // cols):
             first, second = q_ref[0, d], q_ref[1, d]
             block = slice(d * cols, (d + 1) * cols)
-            q_all[:HALF, block] = jnp.concatenate([first[:, :RANK], second[:, :RANK]], axis=1)
-            q_all[HALF:, block] = jnp.concatenate([first[:, RANK:], second[:, RANK:]], axis=1)
+            q_all[:HALF, block] = jnp.where(lane < RANK, first, second)
+            mixed = jnp.where(lane < RANK, second, first)
+            q_all[HALF:, block] = jnp.concatenate([mixed[:, RANK:], mixed[:, :RANK]], axis=1)
         approx = jnp.dot(ortho, q_all[:, span], preferred_element_type=F32)
         error[:, span] = (merged[:, span].astype(F32) - approx).astype(BF16)
         outs[i].start()
@@ -284,6 +297,7 @@
         (shape(BF16, REPLICAS, HALF, cols), shape(BF16, rows, RANK)),
         terms,
         left,
+        scratch=[pltpu.VMEM((18, 8, 2 * RANK), F32)],
     )
     q_all = lax.all_gather(lax.all_to_all(q_copies, DP, 0, 0), "core")
     return rebuild(q_all, ortho, merged, q_warm.shape[1])

time: 98.6 us -> 98.5 us (level)
  no operation moved by 1% of the time
where the time goes in v6:
time: 98.5 us; the launch traced here: 98.1 us
  blocking collectives  83.5 us (85%)
  Pallas kernels  7.88 us (8%)
  starting transfers between devices  6.01 us (6%)
    all_gather x1, blocking collectives, on_device(): warm = lax.all_gather(q_warm.astype(BF16), FSDP, axis=1, tiled=True)  25.4 us
    all_to_all x1, blocking collectives, on_device(): shares = lax.all_to_all(shares, DP, 0, 0)  20.9 us
    all_to_all x1, blocking collectives, on_device(): terms = lax.all_to_all(terms, 'z', 0, 0)  14.8 us
    all_to_all x1, blocking collectives, on_device(): q_all = lax.all_gather(lax.all_to_all(q_copies, DP, 0, 0), 'core')  14.8 us
    all_to_all x1, starting transfers between devices, on_device(): landed = lax.all_to_all(merged.reshape(NEARS, part, col_count), NEAR, 0, 0)  6.01 us
    all_gather x1, blocking collectives, on_device(): q_all = lax.all_gather(lax.all_to_all(q_copies, DP, 0, 0), 'core')  3.95 us
    all_gather x1, blocking collectives, on_device(): lax.all_gather(means, 'core')  3.73 us
    pallas_call x4, Pallas kernels, call(): pl.pallas_call(kernel, out_shape=out, in_specs=[VMEM] * len(operands), ou...  3.55 us
  transfers between devices with their start and end apart: 1, of which 0 were waited for; matrix products, arithmetic and copies ran while one was open for 0% of the time, Pallas kernels for 0%

profile of v6, /device:TPU:1, one launch (start us, length us, event | category | flops | bytes accessed | tf_op | source)
XLA Modules:
  0.0 98.1 jit_solution(6768202637733329612)
XLA Ops:
  0.6 2.4 %shard_map.58.merged = bf16[128,4096]{1,0:T(8,128)(2,1)} custom-call(bf16[1,128,4096]{2,1,0:T(8,128)(2,1)} %grad_hbm.1, bf16[1,128,4096]{2,1,0:T(8,128)(2,1)} %error_hbm.1), custom_call_target="tpu_custom_call" | custom-call | tf_op jit(solution)/shard_map/pallas_call | solution.py:67
  3.0 0.0 copy-start.1
  3.0 6.0 %all-to-all-start = ((bf16[8,16,4096]{2,1,0:T(8,128)(2,1)}), bf16[8,16,4096]{2,1,0:T(8,128)(2,1)S(1)}, u32[]{:S(2)}, u32[]{:S(2)}) async-start(bf16[8,16,4096]{2,1,0:T(8,128)(2,1)} %bitcast.3), calls=%async_computation | async-start | bytes 2097152 | tf_op jit(solution)/shard_map/all_to_all | solution.py:284
  9.0 0.0 copy-done.1
  9.0 25.4 %all_gather.15.warm_ref = bf16[64,4096]{1,0:T(8,128)(2,1)S(1)} all-gather(bf16[64,256]{1,0:T(8,128)(2,1)S(1)} %convert_element_type.3), channel_id=1, replica_groups=mesh['yh'=4,'yl'=2,'x'=4,'z'=8,'core'=2] {'z','core'}, dimensions={1}, use_global_device_ids=true | all-gather | bytes 557056 | tf_op jit(solution)/shard_map/all_gather | solution.py:285
  34.4 0.0 all-to-all-done.landed_ref
  34.4 0.7 shard_map.59
  35.1 20.9 %all_to_all.20.landed_ref = bf16[32,32,128]{2,1,0:T(8,128)(2,1)S(1)} all-to-all(bf16[32,32,128]{2,1,0:T(8,128)(2,1)S(1)} %shard_map.59), channel_id=1, replica_groups=mesh['yh'=4,'yl'=2,'x'=4,'z'=8,'core'=2] {'yh','yl','x'}, dimensions={0} | all-to-all | bytes 524288 | tf_op jit(solution)/shard_map/all_to_all | solution.py:287
  56.0 0.2 shard_map.60
  56.2 3.7 %all-gather = f32[16,24,128]{2,1,0:T(8,128)S(1)} all-gather(f32[8,24,128]{2,1,0:T(8,128)S(1)} %shard_map.60), channel_id=2, replica_groups=mesh['yh'=4,'yl'=2,'x'=4,'z'=8,'core'=2] {'core'}, dimensions={0}, use_global_device_ids=true | all-gather | bytes 294912 | tf_op jit(solution)/shard_map/all_gather | solution.py:292
  59.9 0.4 shard_map.61
  60.3 0.0 copy-start
  60.3 14.8 %all_to_all.21.landed_ref = f32[8,64,128]{2,1,0:T(8,128)S(1)} all-to-all(f32[8,64,128]{2,1,0:T(8,128)S(1)} %get-tuple-element.7), channel_id=1, replica_groups=mesh['yh'=4,'yl'=2,'x'=4,'z'=8,'core'=2] {'z'}, dimensions={0} | all-to-all | bytes 524288 | tf_op jit(solution)/shard_map/all_to_all | solution.py:294
  75.1 2.3 %shard_map.62 = (bf16[32,32,128]{2,1,0:T(8,128)(2,1)S(1)}, bf16[128,64]{1,0:T(8,128)(2,1)S(1)}) custom-call(f32[8,64,128]{2,1,0:T(8,128)S(1)} %all_to_all.21.landed_ref, f32[128,64]{1,0:T(8,128)S(1)} %get-tuple-element.8.left_ref), custom_call_target="tpu_custom_call" | custom-call | tf_op jit(solution)/shard_map/pallas_call | solution.py:27
  77.5 14.8 %all_to_all.22 = bf16[32,32,128]{2,1,0:T(8,128)(2,1)S(1)} all-to-all(bf16[32,32,128]{2,1,0:T(8,128)(2,1)S(1)} %get-tuple-element.9), channel_id=1, replica_groups=mesh['yh'=4,'yl'=2,'x'=4,'z'=8,'core'=2] {'yh','yl','x'}, dimensions={0} | all-to-all | bytes 524288 | tf_op jit(solution)/shard_map/all_to_all | solution.py:302
  92.2 3.9 %all-gather.1 = bf16[64,32,128]{2,1,0:T(8,128)(2,1)S(1)} all-gather(bf16[32,32,128]{2,1,0:T(8,128)(2,1)S(1)} %all_to_all.22), channel_id=3, replica_groups=mesh['yh'=4,'yl'=2,'x'=4,'z'=8,'core'=2] {'core'}, dimensions={0}, use_global_device_ids=true | all-gather | bytes 786432 | tf_op jit(solution)/shard_map/all_gather | solution.py:302
  96.2 0.0 copy-done
  96.2 2.0 %shard_map.63 = (bf16[1,128,4096]{2,1,0:T(8,128)(2,1)}, bf16[128,128]{1,0:T(8,128)(2,1)}, f32[64,256]{1,0:T(8,128)}) custom-call(bf16[2,32,32,128]{3,2,1,0:T(8,128)(2,1)S(1)} %bitcast.4, bf16[128,64]{1,0:T(8,128)(2,1)S(1)} %get-tuple-element.10.ortho_ref, bf16[128,4096]{1,0:T(8,128)(2,1)S(1)} %copy-done), custom_call_target="tpu_custom_call" | custom-call | tf_op jit(solution)/shard_map/pallas_call | solution.py:260
  (1 shorter events, 0.0 us)
Async XLA Ops:
  3.0 6.0 %copy-start.1 = (f32[64,256]{1,0:T(8,128)S(1)}, f32[64,256]{1,0:T(8,128)}, u32[]{:S(2)}) copy-start(f32[64,256]{1,0:T(8,128)} %param.5) | copy-start | bytes 196612
  3.0 31.4 %all-to-all-start = ((bf16[8,16,4096]{2,1,0:T(8,128)(2,1)}), bf16[8,16,4096]{2,1,0:T(8,128)(2,1)S(1)}, u32[]{:S(2)}, u32[]{:S(2)}) async-start(bf16[8,16,4096]{2,1,0:T(8,128)(2,1)} %bitcast.3), calls=%async_computation | async-start | bytes 2097152 | tf_op jit(solution)/shard_map/all_to_all | solution.py:284
  60.3 35.8 %copy-start = (bf16[128,4096]{1,0:T(8,128)(2,1)S(1)}, bf16[128,4096]{1,0:T(8,128)(2,1)}, u32[]{:S(2)}) copy-start(bf16[128,4096]{1,0:T(8,128)(2,1)} %shard_map.58.merged) | copy-start | bytes 3145732

commit v7 on v6

--- a/solution.py
+++ b/solution.py
@@ -219,7 +219,18 @@
 
 
 def rebuild_kernel(
-    q_ref, ortho_ref, merged, error_hbm, own_ref, q_next_ref, q_all, error, out_sems
+    q_ref,
+    ortho_ref,
+    merged,
+    error_hbm,
+    own_hbm,
+    q_next_hbm,
+    q_all,
+    error,
+    own,
+    q_next,
+    out_sems,
+    small_sems,
 ):
     cols = q_ref.shape[3]
     col_count = merged.shape[1]
@@ -232,24 +243,38 @@
         )
     ortho = ortho_ref[...]
     lane = lax.broadcasted_iota(jnp.int32, (HALF, cols), 1)
+
+    def upper_of(d):
+        return jnp.where(lane < RANK, q_ref[0, d], q_ref[1, d])
+
+    def lower_of(d):
+        mixed = jnp.where(lane < RANK, q_ref[1, d], q_ref[0, d])
+        return jnp.concatenate([mixed[:, RANK:], mixed[:, :RANK]], axis=1)
+
+    mine = (lax.axis_index("yh") * YL + lax.axis_index("yl")) * X + lax.axis_index("x")
+    right = jnp.concatenate([upper_of(mine), lower_of(mine)], axis=0)
+    own[...] = jnp.dot(ortho, right, preferred_element_type=F32).astype(BF16)
+    own_copy = pltpu.make_async_copy(own, own_hbm, small_sems.at[0])
+    own_copy.start()
+    count = q_next.shape[1] // cols
+    first = (lax.axis_index("z") * CORES + lax.axis_index("core")) * count
+    for i in range(count):
+        q_next[:HALF, i * cols : (i + 1) * cols] = upper_of(first + i).astype(F32)
+        q_next[HALF:, i * cols : (i + 1) * cols] = lower_of(first + i).astype(F32)
+    q_next_copy = pltpu.make_async_copy(q_next, q_next_hbm, small_sems.at[1])
+    q_next_copy.start()
+
     for i in range(SPANS):
         span = slice(i * wide, (i + 1) * wide)
         for d in range(i * wide // cols, (i + 1) * wide // cols):
-            first, second = q_ref[0, d], q_ref[1, d]
             block = slice(d * cols, (d + 1) * cols)
-            q_all[:HALF, block] = jnp.where(lane < RANK, first, second)
-            mixed = jnp.where(lane < RANK, second, first)
-            q_all[HALF:, block] = jnp.concatenate([mixed[:, RANK:], mixed[:, :RANK]], axis=1)
+            q_all[:HALF, block] = upper_of(d)
+            q_all[HALF:, block] = lower_of(d)
         approx = jnp.dot(ortho, q_all[:, span], preferred_element_type=F32)
         error[:, span] = (merged[:, span].astype(F32) - approx).astype(BF16)
         outs[i].start()
-
-    own = (lax.axis_index("yh") * YL + lax.axis_index("yl")) * X + lax.axis_index("x")
-    right = q_all[:, pl.ds(pl.multiple_of(own * cols, cols), cols)]
-    own_ref[...] = jnp.dot(ortho, right, preferred_element_type=F32).astype(BF16)
-    shard = q_next_ref.shape[1]
-    first = (lax.axis_index("z") * CORES + lax.axis_index("core")) * shard
-    q_next_ref[...] = q_all[:, pl.ds(pl.multiple_of(first, shard), shard)].astype(F32)
+    own_copy.wait()
+    q_next_copy.wait()
     for i in range(SPANS):
         outs[i].wait()
 
@@ -265,11 +290,14 @@
             shape(F32, RANK, shard),
         ),
         in_specs=[VMEM, VMEM, VMEM],
-        out_specs=[ANY, VMEM, VMEM],
+        out_specs=[ANY, ANY, ANY],
         scratch_shapes=[
             pltpu.VMEM((RANK, col_count), BF16),
             pltpu.VMEM((rows, col_count), BF16),
+            pltpu.VMEM((rows, cols), BF16),
+            pltpu.VMEM((RANK, shard), F32),
             pltpu.SemaphoreType.DMA((SPANS,)),
+            pltpu.SemaphoreType.DMA((2,)),
         ],
         compiler_params=pltpu.CompilerParams(vmem_limit_bytes=LIMIT),
     )(q_all, ortho, merged)

time: 98.5 us -> 97.9 us (level)
  no operation moved by 1% of the time
where the time goes in v7:
time: 97.9 us; the launch traced here: 97.5 us
  blocking collectives  83.5 us (85%)
  Pallas kernels  7.27 us (7%)
  starting transfers between devices  6.01 us (6%)
    all_gather x1, blocking collectives, on_device(): warm = lax.all_gather(q_warm.astype(BF16), FSDP, axis=1, tiled=True)  25.4 us
    all_to_all x1, blocking collectives, on_device(): shares = lax.all_to_all(shares, DP, 0, 0)  20.9 us
    all_to_all x1, blocking collectives, on_device(): terms = lax.all_to_all(terms, 'z', 0, 0)  14.8 us
    all_to_all x1, blocking collectives, on_device(): q_all = lax.all_gather(lax.all_to_all(q_copies, DP, 0, 0), 'core')  14.8 us
    all_to_all x1, starting transfers between devices, on_device(): landed = lax.all_to_all(merged.reshape(NEARS, part, col_count), NEAR, 0, 0)  6.01 us
    all_gather x1, blocking collectives, on_device(): q_all = lax.all_gather(lax.all_to_all(q_copies, DP, 0, 0), 'core')  3.95 us
    all_gather x1, blocking collectives, on_device(): lax.all_gather(means, 'core')  3.73 us
    pallas_call x4, Pallas kernels, call(): pl.pallas_call(kernel, out_shape=out, in_specs=[VMEM] * len(operands), ou...  3.55 us
  transfers between devices with their start and end apart: 1, of which 0 were waited for; matrix products, arithmetic and copies ran while one was open for 0% of the time, Pallas kernels for 0%

profile of v7, /device:TPU:1, one launch (start us, length us, event | category | flops | bytes accessed | tf_op | source)
XLA Modules:
  0.0 97.5 jit_solution(7560567686101864123)
XLA Ops:
  0.6 2.4 %shard_map.58.merged = bf16[128,4096]{1,0:T(8,128)(2,1)} custom-call(bf16[1,128,4096]{2,1,0:T(8,128)(2,1)} %grad_hbm.1, bf16[1,128,4096]{2,1,0:T(8,128)(2,1)} %error_hbm.1), custom_call_target="tpu_custom_call" | custom-call | tf_op jit(solution)/shard_map/pallas_call | solution.py:67
  3.0 0.0 copy-start.1
  3.0 6.0 %all-to-all-start = ((bf16[8,16,4096]{2,1,0:T(8,128)(2,1)}), bf16[8,16,4096]{2,1,0:T(8,128)(2,1)S(1)}, u32[]{:S(2)}, u32[]{:S(2)}) async-start(bf16[8,16,4096]{2,1,0:T(8,128)(2,1)} %bitcast.3), calls=%async_computation | async-start | bytes 2097152 | tf_op jit(solution)/shard_map/all_to_all | solution.py:312
  9.0 0.0 copy-done.1
  9.0 25.4 %all_gather.15.warm_ref = bf16[64,4096]{1,0:T(8,128)(2,1)S(1)} all-gather(bf16[64,256]{1,0:T(8,128)(2,1)S(1)} %convert_element_type.3), channel_id=1, replica_groups=mesh['yh'=4,'yl'=2,'x'=4,'z'=8,'core'=2] {'z','core'}, dimensions={1}, use_global_device_ids=true | all-gather | bytes 557056 | tf_op jit(solution)/shard_map/all_gather | solution.py:313
  34.4 0.0 all-to-all-done.landed_ref
  34.4 0.7 shard_map.59
  35.1 20.9 %all_to_all.20.landed_ref = bf16[32,32,128]{2,1,0:T(8,128)(2,1)S(1)} all-to-all(bf16[32,32,128]{2,1,0:T(8,128)(2,1)S(1)} %shard_map.59), channel_id=1, replica_groups=mesh['yh'=4,'yl'=2,'x'=4,'z'=8,'core'=2] {'yh','yl','x'}, dimensions={0} | all-to-all | bytes 524288 | tf_op jit(solution)/shard_map/all_to_all | solution.py:315
  56.0 0.2 shard_map.60
  56.2 3.7 %all-gather = f32[16,24,128]{2,1,0:T(8,128)S(1)} all-gather(f32[8,24,128]{2,1,0:T(8,128)S(1)} %shard_map.60), channel_id=2, replica_groups=mesh['yh'=4,'yl'=2,'x'=4,'z'=8,'core'=2] {'core'}, dimensions={0}, use_global_device_ids=true | all-gather | bytes 294912 | tf_op jit(solution)/shard_map/all_gather | solution.py:320
  59.9 0.4 shard_map.61
  60.3 0.0 copy-start
  60.3 14.8 %all_to_all.21.landed_ref = f32[8,64,128]{2,1,0:T(8,128)S(1)} all-to-all(f32[8,64,128]{2,1,0:T(8,128)S(1)} %get-tuple-element.7), channel_id=1, replica_groups=mesh['yh'=4,'yl'=2,'x'=4,'z'=8,'core'=2] {'z'}, dimensions={0} | all-to-all | bytes 524288 | tf_op jit(solution)/shard_map/all_to_all | solution.py:322
  75.1 2.3 %shard_map.62 = (bf16[32,32,128]{2,1,0:T(8,128)(2,1)S(1)}, bf16[128,64]{1,0:T(8,128)(2,1)S(1)}) custom-call(f32[8,64,128]{2,1,0:T(8,128)S(1)} %all_to_all.21.landed_ref, f32[128,64]{1,0:T(8,128)S(1)} %get-tuple-element.8.left_ref), custom_call_target="tpu_custom_call" | custom-call | tf_op jit(solution)/shard_map/pallas_call | solution.py:27
  77.5 14.8 %all_to_all.22 = bf16[32,32,128]{2,1,0:T(8,128)(2,1)S(1)} all-to-all(bf16[32,32,128]{2,1,0:T(8,128)(2,1)S(1)} %get-tuple-element.9), channel_id=1, replica_groups=mesh['yh'=4,'yl'=2,'x'=4,'z'=8,'core'=2] {'yh','yl','x'}, dimensions={0} | all-to-all | bytes 524288 | tf_op jit(solution)/shard_map/all_to_all | solution.py:330
  92.2 3.9 %all-gather.1 = bf16[64,32,128]{2,1,0:T(8,128)(2,1)S(1)} all-gather(bf16[32,32,128]{2,1,0:T(8,128)(2,1)S(1)} %all_to_all.22), channel_id=3, replica_groups=mesh['yh'=4,'yl'=2,'x'=4,'z'=8,'core'=2] {'core'}, dimensions={0}, use_global_device_ids=true | all-gather | bytes 786432 | tf_op jit(solution)/shard_map/all_gather | solution.py:330
  96.2 0.0 copy-done
  96.2 1.3 %shard_map.63 = (bf16[1,128,4096]{2,1,0:T(8,128)(2,1)}, bf16[128,128]{1,0:T(8,128)(2,1)}, f32[64,256]{1,0:T(8,128)}) custom-call(bf16[2,32,32,128]{3,2,1,0:T(8,128)(2,1)S(1)} %bitcast.4, bf16[128,64]{1,0:T(8,128)(2,1)S(1)} %get-tuple-element.10.ortho_ref, bf16[128,4096]{1,0:T(8,128)(2,1)S(1)} %copy-done), custom_call_target="tpu_custom_call" | custom-call | tf_op jit(solution)/shard_map/pallas_call | solution.py:285
  (1 shorter events, 0.0 us)
Async XLA Ops:
  3.0 6.0 %copy-start.1 = (f32[64,256]{1,0:T(8,128)S(1)}, f32[64,256]{1,0:T(8,128)}, u32[]{:S(2)}) copy-start(f32[64,256]{1,0:T(8,128)} %param.5) | copy-start | bytes 196612
  3.0 31.4 %all-to-all-start = ((bf16[8,16,4096]{2,1,0:T(8,128)(2,1)}), bf16[8,16,4096]{2,1,0:T(8,128)(2,1)S(1)}, u32[]{:S(2)}, u32[]{:S(2)}) async-start(bf16[8,16,4096]{2,1,0:T(8,128)(2,1)} %bitcast.3), calls=%async_computation | async-start | bytes 2097152 | tf_op jit(solution)/shard_map/all_to_all | solution.py:312
  60.3 35.8 %copy-start = (bf16[128,4096]{1,0:T(8,128)(2,1)S(1)}, bf16[128,4096]{1,0:T(8,128)(2,1)}, u32[]{:S(2)}) copy-start(bf16[128,4096]{1,0:T(8,128)(2,1)} %shard_map.58.merged) | copy-start | bytes 3145732

commit v8 on v7

--- a/solution.py
+++ b/solution.py
@@ -138,20 +138,42 @@
         precision=EXACT,
         preferred_element_type=F32,
     )
+    quarter = HALF // 2
+    third, fourth = terms[HALF : HALF + quarter], terms[HALF + quarter :]
+    middle = jnp.concatenate([third[:, HALF:RANK], fourth[:, HALF:RANK], third[:, RANK:]], axis=1)
+    last = jnp.concatenate([fourth[: quarter // 2, RANK:], fourth[quarter // 2 :, RANK:]], axis=1)
     for z in range(Z):
-        out_ref[z] = terms
+        out_ref[z, :HALF] = terms[:HALF]
+        out_ref[z, HALF : HALF + quarter] = middle
+        out_ref[z, HALF + quarter :] = last
 
 
 def factor_kernel(landed_ref, left_ref, q_ref, ortho_ref, held):
     sums = landed_ref[0]
     for z in range(1, Z):
         sums = sums + landed_ref[z]
+    upper = sums[:HALF]
+    middle = sums[HALF : HALF + HALF // 2]
+    last = sums[HALF + HALF // 2 :]
+    across = upper.T[HALF:RANK]
+    rest = jnp.zeros((HALF // 2, RANK), F32)
+    gram = jnp.concatenate(
+        [
+            upper,
+            jnp.concatenate([across[: HALF // 2], middle[:, :HALF], rest], axis=1),
+            jnp.concatenate([across[HALF // 2 :], middle[:, HALF:RANK], rest], axis=1),
+        ],
+        axis=0,
+    )
+    q_sum = jnp.concatenate(
+        [upper[:, RANK:], middle[:, RANK:], last[:, :RANK], last[:, RANK:]], axis=0
+    )
     lane = lax.broadcasted_iota(jnp.int32, (8, 2 * RANK), 1)
     sub = lax.broadcasted_iota(jnp.int32, (8, 2 * RANK), 0)
     blocks = []
     for b in range(RANK // 8):
         unit = (lane == sub + RANK + 8 * b).astype(F32)
-        blocks.append(jnp.where(lane < RANK, sums[8 * b : 8 * b + 8], unit))
+        blocks.append(jnp.where(lane < RANK, gram[8 * b : 8 * b + 8], unit))
 
     def lane_copy(value, column):
         return jnp.broadcast_to(value[:, column : column + 1], value.shape)
@@ -199,13 +221,12 @@
             blocks[t] = blocks[t] - update
     inverse = jnp.concatenate(inverse_rows, axis=0)[:, RANK:]
 
-    q_sum = sums[:, RANK:]
     q_mine = jnp.dot(inverse, q_sum, precision=EXACT, preferred_element_type=F32).astype(BF16)
-    upper, lower = q_mine[:HALF], q_mine[HALF:]
+    q_upper, q_lower = q_mine[:HALF], q_mine[HALF:]
     q_mine = jnp.where(
         lax.axis_index("core") == 0,
-        jnp.concatenate([upper, lower], axis=1),
-        jnp.concatenate([lower, upper], axis=1),
+        jnp.concatenate([q_upper, q_lower], axis=1),
+        jnp.concatenate([q_lower, q_upper], axis=1),
     )
     for peer in range(q_ref.shape[0]):
         q_ref[peer] = q_mine
@@ -316,7 +337,7 @@
     means = call(mean_kernel, shape(F32, NEARS, part + part // 2, cols), shares)
     terms, left = call(
         terms_kernel,
-        (shape(F32, Z, RANK, 2 * RANK), shape(F32, rows, RANK)),
+        (shape(F32, Z, RANK - 8, 2 * RANK), shape(F32, rows, RANK)),
         lax.all_gather(means, "core"),
     )
     terms = lax.all_to_all(terms, "z", 0, 0)

time: 97.9 us -> 97 us (level)
    all_gather x1, blocking collectives: 3.95 us -> 5.1 us  [on_device(): q_all = lax.all_gather(lax.all_to_all(q_copies, DP, 0, 0), 'core')]
    all_to_all x1, blocking collectives: 14.8 us -> 13.7 us  [on_device(): terms = lax.all_to_all(terms, 'z', 0, 0)]
where the time goes in v8:
time: 97 us; the launch traced here: 96.7 us
  blocking collectives  82.6 us (85%)
  Pallas kernels  7.39 us (8%)
  starting transfers between devices  6.01 us (6%)
    all_gather x1, blocking collectives, on_device(): warm = lax.all_gather(q_warm.astype(BF16), FSDP, axis=1, tiled=True)  25.4 us
    all_to_all x1, blocking collectives, on_device(): shares = lax.all_to_all(shares, DP, 0, 0)  20.9 us
    all_to_all x1, blocking collectives, on_device(): q_all = lax.all_gather(lax.all_to_all(q_copies, DP, 0, 0), 'core')  13.8 us
    all_to_all x1, blocking collectives, on_device(): terms = lax.all_to_all(terms, 'z', 0, 0)  13.7 us
    all_to_all x1, starting transfers between devices, on_device(): landed = lax.all_to_all(merged.reshape(NEARS, part, col_count), NEAR, 0, 0)  6.01 us
    all_gather x1, blocking collectives, on_device(): q_all = lax.all_gather(lax.all_to_all(q_copies, DP, 0, 0), 'core')  5.1 us
    all_gather x1, blocking collectives, on_device(): lax.all_gather(means, 'core')  3.73 us
    pallas_call x4, Pallas kernels, call(): pl.pallas_call(kernel, out_shape=out, in_specs=[VMEM] * len(operands), ou...  3.67 us
  transfers between devices with their start and end apart: 1, of which 0 were waited for; matrix products, arithmetic and copies ran while one was open for 0% of the time, Pallas kernels for 0%

profile of v8, /device:TPU:1, one launch (start us, length us, event | category | flops | bytes accessed | tf_op | source)
XLA Modules:
  0.0 96.7 jit_solution(6448297010224079212)
XLA Ops:
  0.6 2.4 %shard_map.58.merged = bf16[128,4096]{1,0:T(8,128)(2,1)} custom-call(bf16[1,128,4096]{2,1,0:T(8,128)(2,1)} %grad_hbm.1, bf16[1,128,4096]{2,1,0:T(8,128)(2,1)} %error_hbm.1), custom_call_target="tpu_custom_call" | custom-call | tf_op jit(solution)/shard_map/pallas_call | solution.py:67
  3.0 0.0 copy-start.1
  3.0 6.0 %all-to-all-start = ((bf16[8,16,4096]{2,1,0:T(8,128)(2,1)}), bf16[8,16,4096]{2,1,0:T(8,128)(2,1)S(1)}, u32[]{:S(2)}, u32[]{:S(2)}) async-start(bf16[8,16,4096]{2,1,0:T(8,128)(2,1)} %bitcast.3), calls=%async_computation | async-start | bytes 2097152 | tf_op jit(solution)/shard_map/all_to_all | solution.py:333
  9.0 0.0 copy-done.1
  9.0 25.4 %all_gather.15.warm_ref = bf16[64,4096]{1,0:T(8,128)(2,1)S(1)} all-gather(bf16[64,256]{1,0:T(8,128)(2,1)S(1)} %convert_element_type.3), channel_id=1, replica_groups=mesh['yh'=4,'yl'=2,'x'=4,'z'=8,'core'=2] {'z','core'}, dimensions={1}, use_global_device_ids=true | all-gather | bytes 557056 | tf_op jit(solution)/shard_map/all_gather | solution.py:334
  34.4 0.0 all-to-all-done.landed_ref
  34.4 0.7 shard_map.59
  35.1 20.9 %all_to_all.20.landed_ref = bf16[32,32,128]{2,1,0:T(8,128)(2,1)S(1)} all-to-all(bf16[32,32,128]{2,1,0:T(8,128)(2,1)S(1)} %shard_map.59), channel_id=1, replica_groups=mesh['yh'=4,'yl'=2,'x'=4,'z'=8,'core'=2] {'yh','yl','x'}, dimensions={0} | all-to-all | bytes 524288 | tf_op jit(solution)/shard_map/all_to_all | solution.py:336
  56.0 0.2 shard_map.60
  56.2 3.7 %all-gather = f32[16,24,128]{2,1,0:T(8,128)S(1)} all-gather(f32[8,24,128]{2,1,0:T(8,128)S(1)} %shard_map.60), channel_id=2, replica_groups=mesh['yh'=4,'yl'=2,'x'=4,'z'=8,'core'=2] {'core'}, dimensions={0}, use_global_device_ids=true | all-gather | bytes 294912 | tf_op jit(solution)/shard_map/all_gather | solution.py:341
  59.9 0.5 shard_map.61
  60.4 0.0 copy-start
  60.4 13.7 %all_to_all.21.landed_ref = f32[8,56,128]{2,1,0:T(8,128)S(1)} all-to-all(f32[8,56,128]{2,1,0:T(8,128)S(1)} %get-tuple-element.7), channel_id=1, replica_groups=mesh['yh'=4,'yl'=2,'x'=4,'z'=8,'core'=2] {'z'}, dimensions={0} | all-to-all | bytes 458752 | tf_op jit(solution)/shard_map/all_to_all | solution.py:343
  74.1 2.4 %shard_map.62 = (bf16[32,32,128]{2,1,0:T(8,128)(2,1)S(1)}, bf16[128,64]{1,0:T(8,128)(2,1)S(1)}) custom-call(f32[8,56,128]{2,1,0:T(8,128)S(1)} %all_to_all.21.landed_ref, f32[128,64]{1,0:T(8,128)S(1)} %get-tuple-element.8.left_ref), custom_call_target="tpu_custom_call" | custom-call | tf_op jit(solution)/shard_map/pallas_call | solution.py:27
  76.4 13.8 %all_to_all.22 = bf16[32,32,128]{2,1,0:T(8,128)(2,1)S(1)} all-to-all(bf16[32,32,128]{2,1,0:T(8,128)(2,1)S(1)} %get-tuple-element.9), channel_id=1, replica_groups=mesh['yh'=4,'yl'=2,'x'=4,'z'=8,'core'=2] {'yh','yl','x'}, dimensions={0} | all-to-all | bytes 524288 | tf_op jit(solution)/shard_map/all_to_all | solution.py:351
  90.2 5.1 %all-gather.1 = bf16[64,32,128]{2,1,0:T(8,128)(2,1)S(1)} all-gather(bf16[32,32,128]{2,1,0:T(8,128)(2,1)S(1)} %all_to_all.22), channel_id=3, replica_groups=mesh['yh'=4,'yl'=2,'x'=4,'z'=8,'core'=2] {'core'}, dimensions={0}, use_global_device_ids=true | all-gather | bytes 786432 | tf_op jit(solution)/shard_map/all_gather | solution.py:351
  95.3 0.0 copy-done
  95.3 1.4 %shard_map.63 = (bf16[1,128,4096]{2,1,0:T(8,128)(2,1)}, bf16[128,128]{1,0:T(8,128)(2,1)}, f32[64,256]{1,0:T(8,128)}) custom-call(bf16[2,32,32,128]{3,2,1,0:T(8,128)(2,1)S(1)} %bitcast.4, bf16[128,64]{1,0:T(8,128)(2,1)S(1)} %get-tuple-element.10.ortho_ref, bf16[128,4096]{1,0:T(8,128)(2,1)S(1)} %copy-done), custom_call_target="tpu_custom_call" | custom-call | tf_op jit(solution)/shard_map/pallas_call | solution.py:306
  (1 shorter events, 0.0 us)
Async XLA Ops:
  3.0 6.0 %copy-start.1 = (f32[64,256]{1,0:T(8,128)S(1)}, f32[64,256]{1,0:T(8,128)}, u32[]{:S(2)}) copy-start(f32[64,256]{1,0:T(8,128)} %param.5) | copy-start | bytes 196612
  3.0 31.4 %all-to-all-start = ((bf16[8,16,4096]{2,1,0:T(8,128)(2,1)}), bf16[8,16,4096]{2,1,0:T(8,128)(2,1)S(1)}, u32[]{:S(2)}, u32[]{:S(2)}) async-start(bf16[8,16,4096]{2,1,0:T(8,128)(2,1)} %bitcast.3), calls=%async_computation | async-start | bytes 2097152 | tf_op jit(solution)/shard_map/all_to_all | solution.py:333
  60.4 35.0 %copy-start = (bf16[128,4096]{1,0:T(8,128)(2,1)S(1)}, bf16[128,4096]{1,0:T(8,128)(2,1)}, u32[]{:S(2)}) copy-start(bf16[128,4096]{1,0:T(8,128)(2,1)} %shard_map.58.merged) | copy-start | bytes 3145732

commit v9 on v8

--- a/solution.py
+++ b/solution.py
@@ -10,8 +10,15 @@
 DP = ("yh", "yl", "x")
 FSDP = ("z", "core")
 NEARS = YL * X
-CUTS = 4
-SPANS = 4
+CUTS = (3, 3, 1, 1)
+SPANS = (1, 2, 2, 2, 1)
+
+
+def pieces(sizes, whole):
+    unit = whole // sum(sizes)
+    return [(sum(sizes[:i]) * unit, sizes[i] * unit) for i in range(len(sizes))]
+
+
 REPLICAS = YH * YL * X
 RANK = 64
 HALF = RANK // 2
@@ -39,10 +46,10 @@
 
 
 def merge_kernel(grad_hbm, error_hbm, merged_hbm, grad, error, merged, in_sems, out_sems):
-    part = merged.shape[0] // CUTS
+    cuts = pieces(CUTS, merged.shape[0])
     copies = []
-    for i in range(CUTS):
-        span = pl.ds(i * part, part)
+    for i, (start, size) in enumerate(cuts):
+        span = pl.ds(start, size)
         copies.append(
             (
                 pltpu.make_async_copy(grad_hbm.at[0, span], grad.at[span], in_sems.at[0, i]),
@@ -52,14 +59,14 @@
         )
         copies[i][0].start()
         copies[i][1].start()
-    for i in range(CUTS):
+    for i, (start, size) in enumerate(cuts):
         copies[i][0].wait()
         copies[i][1].wait()
-        span = pl.ds(i * part, part)
+        span = pl.ds(start, size)
         merged[span] = (grad[span].astype(F32) + error[span].astype(F32)).astype(BF16)
         copies[i][2].start()
-    for i in range(CUTS):
-        copies[i][2].wait()
+    for copy in copies:
+        copy[2].wait()
 
 
 def merge(grad, error):
@@ -70,7 +77,7 @@
         in_specs=[ANY, ANY],
         out_specs=ANY,
         scratch_shapes=[pltpu.VMEM((rows, col_count), BF16)] * 3
-        + [pltpu.SemaphoreType.DMA((2, CUTS)), pltpu.SemaphoreType.DMA((CUTS,))],
+        + [pltpu.SemaphoreType.DMA((2, len(CUTS))), pltpu.SemaphoreType.DMA((len(CUTS),))],
         compiler_params=pltpu.CompilerParams(vmem_limit_bytes=60 * 1024 * 1024),
     )(grad, error)
 
@@ -255,10 +262,10 @@
 ):
     cols = q_ref.shape[3]
     col_count = merged.shape[1]
-    wide = col_count // SPANS
+    spans = pieces(SPANS, col_count)
     outs = []
-    for i in range(SPANS):
-        span = pl.ds(i * wide, wide)
+    for i, (start, wide) in enumerate(spans):
+        span = pl.ds(start, wide)
         outs.append(
             pltpu.make_async_copy(error.at[:, span], error_hbm.at[0, :, span], out_sems.at[i])
         )
@@ -285,9 +292,9 @@
     q_next_copy = pltpu.make_async_copy(q_next, q_next_hbm, small_sems.at[1])
     q_next_copy.start()
 
-    for i in range(SPANS):
-        span = slice(i * wide, (i + 1) * wide)
-        for d in range(i * wide // cols, (i + 1) * wide // cols):
+    for i, (start, wide) in enumerate(spans):
+        span = slice(start, start + wide)
+        for d in range(start // cols, (start + wide) // cols):
             block = slice(d * cols, (d + 1) * cols)
             q_all[:HALF, block] = upper_of(d)
             q_all[HALF:, block] = lower_of(d)
@@ -296,8 +303,8 @@
         outs[i].start()
     own_copy.wait()
     q_next_copy.wait()
-    for i in range(SPANS):
-        outs[i].wait()
+    for out in outs:
+        out.wait()
 
 
 def rebuild(q_all, ortho, merged, shard):
@@ -317,7 +324,7 @@
             pltpu.VMEM((rows, col_count), BF16),
             pltpu.VMEM((rows, cols), BF16),
             pltpu.VMEM((RANK, shard), F32),
-            pltpu.SemaphoreType.DMA((SPANS,)),
+            pltpu.SemaphoreType.DMA((len(SPANS),)),
             pltpu.SemaphoreType.DMA((2,)),
         ],
         compiler_params=pltpu.CompilerParams(vmem_limit_bytes=LIMIT),

time: 97 us -> 97.1 us (level)
  no operation moved by 1% of the time
where the time goes in v9:
time: 97.1 us; the launch traced here: 96.7 us
  blocking collectives  82.6 us (85%)
  Pallas kernels  7.4 us (8%)
  starting transfers between devices  6.01 us (6%)
    all_gather x1, blocking collectives, on_device(): warm = lax.all_gather(q_warm.astype(BF16), FSDP, axis=1, tiled=True)  25.4 us
    all_to_all x1, blocking collectives, on_device(): shares = lax.all_to_all(shares, DP, 0, 0)  20.9 us
    all_to_all x1, blocking collectives, on_device(): q_all = lax.all_gather(lax.all_to_all(q_copies, DP, 0, 0), 'core')  13.8 us
    all_to_all x1, blocking collectives, on_device(): terms = lax.all_to_all(terms, 'z', 0, 0)  13.7 us
    all_to_all x1, starting transfers between devices, on_device(): landed = lax.all_to_all(merged.reshape(NEARS, part, col_count), NEAR, 0, 0)  6.01 us
    all_gather x1, blocking collectives, on_device(): q_all = lax.all_gather(lax.all_to_all(q_copies, DP, 0, 0), 'core')  5.09 us
    all_gather x1, blocking collectives, on_device(): lax.all_gather(means, 'core')  3.73 us
    pallas_call x4, Pallas kernels, call(): pl.pallas_call(kernel, out_shape=out, in_specs=[VMEM] * len(operands), ou...  3.67 us
  transfers between devices with their start and end apart: 1, of which 0 were waited for; matrix products, arithmetic and copies ran while one was open for 0% of the time, Pallas kernels for 0%

profile of v9, /device:TPU:1, one launch (start us, length us, event | category | flops | bytes accessed | tf_op | source)
XLA Modules:
  0.0 96.7 jit_solution(17052970255207182112)
XLA Ops:
  0.6 2.4 %shard_map.58.merged = bf16[128,4096]{1,0:T(8,128)(2,1)} custom-call(bf16[1,128,4096]{2,1,0:T(8,128)(2,1)} %grad_hbm.1, bf16[1,128,4096]{2,1,0:T(8,128)(2,1)} %error_hbm.1), custom_call_target="tpu_custom_call" | custom-call | tf_op jit(solution)/shard_map/pallas_call | solution.py:74
  3.0 0.0 copy-start.1
  3.0 6.0 %all-to-all-start = ((bf16[8,16,4096]{2,1,0:T(8,128)(2,1)}), bf16[8,16,4096]{2,1,0:T(8,128)(2,1)S(1)}, u32[]{:S(2)}, u32[]{:S(2)}) async-start(bf16[8,16,4096]{2,1,0:T(8,128)(2,1)} %bitcast.3), calls=%async_computation | async-start | bytes 2097152 | tf_op jit(solution)/shard_map/all_to_all | solution.py:340
  9.0 0.0 copy-done.1
  9.0 25.4 %all_gather.15.warm_ref = bf16[64,4096]{1,0:T(8,128)(2,1)S(1)} all-gather(bf16[64,256]{1,0:T(8,128)(2,1)S(1)} %convert_element_type.3), channel_id=1, replica_groups=mesh['yh'=4,'yl'=2,'x'=4,'z'=8,'core'=2] {'z','core'}, dimensions={1}, use_global_device_ids=true | all-gather | bytes 557056 | tf_op jit(solution)/shard_map/all_gather | solution.py:341
  34.4 0.0 all-to-all-done.landed_ref
  34.4 0.7 shard_map.59
  35.2 20.9 %all_to_all.20.landed_ref = bf16[32,32,128]{2,1,0:T(8,128)(2,1)S(1)} all-to-all(bf16[32,32,128]{2,1,0:T(8,128)(2,1)S(1)} %shard_map.59), channel_id=1, replica_groups=mesh['yh'=4,'yl'=2,'x'=4,'z'=8,'core'=2] {'yh','yl','x'}, dimensions={0} | all-to-all | bytes 524288 | tf_op jit(solution)/shard_map/all_to_all | solution.py:343
  56.1 0.2 shard_map.60
  56.2 3.7 %all-gather = f32[16,24,128]{2,1,0:T(8,128)S(1)} all-gather(f32[8,24,128]{2,1,0:T(8,128)S(1)} %shard_map.60), channel_id=2, replica_groups=mesh['yh'=4,'yl'=2,'x'=4,'z'=8,'core'=2] {'core'}, dimensions={0}, use_global_device_ids=true | all-gather | bytes 294912 | tf_op jit(solution)/shard_map/all_gather | solution.py:348
  59.9 0.5 shard_map.61
  60.4 0.0 copy-start
  60.4 13.7 %all_to_all.21.landed_ref = f32[8,56,128]{2,1,0:T(8,128)S(1)} all-to-all(f32[8,56,128]{2,1,0:T(8,128)S(1)} %get-tuple-element.7), channel_id=1, replica_groups=mesh['yh'=4,'yl'=2,'x'=4,'z'=8,'core'=2] {'z'}, dimensions={0} | all-to-all | bytes 458752 | tf_op jit(solution)/shard_map/all_to_all | solution.py:350
  74.1 2.3 %shard_map.62 = (bf16[32,32,128]{2,1,0:T(8,128)(2,1)S(1)}, bf16[128,64]{1,0:T(8,128)(2,1)S(1)}) custom-call(f32[8,56,128]{2,1,0:T(8,128)S(1)} %all_to_all.21.landed_ref, f32[128,64]{1,0:T(8,128)S(1)} %get-tuple-element.8.left_ref), custom_call_target="tpu_custom_call" | custom-call | tf_op jit(solution)/shard_map/pallas_call | solution.py:34
  76.4 13.8 %all_to_all.22 = bf16[32,32,128]{2,1,0:T(8,128)(2,1)S(1)} all-to-all(bf16[32,32,128]{2,1,0:T(8,128)(2,1)S(1)} %get-tuple-element.9), channel_id=1, replica_groups=mesh['yh'=4,'yl'=2,'x'=4,'z'=8,'core'=2] {'yh','yl','x'}, dimensions={0} | all-to-all | bytes 524288 | tf_op jit(solution)/shard_map/all_to_all | solution.py:358
  90.3 5.1 %all-gather.1 = bf16[64,32,128]{2,1,0:T(8,128)(2,1)S(1)} all-gather(bf16[32,32,128]{2,1,0:T(8,128)(2,1)S(1)} %all_to_all.22), channel_id=3, replica_groups=mesh['yh'=4,'yl'=2,'x'=4,'z'=8,'core'=2] {'core'}, dimensions={0}, use_global_device_ids=true | all-gather | bytes 786432 | tf_op jit(solution)/shard_map/all_gather | solution.py:358
  95.3 0.0 copy-done
  95.3 1.4 %shard_map.63 = (bf16[1,128,4096]{2,1,0:T(8,128)(2,1)}, bf16[128,128]{1,0:T(8,128)(2,1)}, f32[64,256]{1,0:T(8,128)}) custom-call(bf16[2,32,32,128]{3,2,1,0:T(8,128)(2,1)S(1)} %bitcast.4, bf16[128,64]{1,0:T(8,128)(2,1)S(1)} %get-tuple-element.10.ortho_ref, bf16[128,4096]{1,0:T(8,128)(2,1)S(1)} %copy-done), custom_call_target="tpu_custom_call" | custom-call | tf_op jit(solution)/shard_map/pallas_call | solution.py:313
  (1 shorter events, 0.0 us)
Async XLA Ops:
  3.0 6.0 %copy-start.1 = (f32[64,256]{1,0:T(8,128)S(1)}, f32[64,256]{1,0:T(8,128)}, u32[]{:S(2)}) copy-start(f32[64,256]{1,0:T(8,128)} %param.5) | copy-start | bytes 196612
  3.0 31.4 %all-to-all-start = ((bf16[8,16,4096]{2,1,0:T(8,128)(2,1)}), bf16[8,16,4096]{2,1,0:T(8,128)(2,1)S(1)}, u32[]{:S(2)}, u32[]{:S(2)}) async-start(bf16[8,16,4096]{2,1,0:T(8,128)(2,1)} %bitcast.3), calls=%async_computation | async-start | bytes 2097152 | tf_op jit(solution)/shard_map/all_to_all | solution.py:340
  60.4 35.0 %copy-start = (bf16[128,4096]{1,0:T(8,128)(2,1)S(1)}, bf16[128,4096]{1,0:T(8,128)(2,1)}, u32[]{:S(2)}) copy-start(bf16[128,4096]{1,0:T(8,128)(2,1)} %shard_map.58.merged) | copy-start | bytes 3145732

commit v10 on v9

--- a/solution.py
+++ b/solution.py
@@ -45,7 +45,10 @@
     return jax.ShapeDtypeStruct(dims, dtype)
 
 
-def merge_kernel(grad_hbm, error_hbm, merged_hbm, grad, error, merged, in_sems, out_sems):
+def merge_kernel(
+    grad_hbm, error_hbm, q_hbm, merged_hbm, warm_ref, grad, error, merged, q, in_sems, out_sems, q_sem
+):
+    q_copy = pltpu.make_async_copy(q_hbm, q, q_sem)
     cuts = pieces(CUTS, merged.shape[0])
     copies = []
     for i, (start, size) in enumerate(cuts):
@@ -59,27 +62,35 @@
         )
         copies[i][0].start()
         copies[i][1].start()
+    q_copy.start()
     for i, (start, size) in enumerate(cuts):
         copies[i][0].wait()
         copies[i][1].wait()
         span = pl.ds(start, size)
         merged[span] = (grad[span].astype(F32) + error[span].astype(F32)).astype(BF16)
         copies[i][2].start()
+    q_copy.wait()
+    warm_ref[...] = q[...].astype(BF16)
     for copy in copies:
         copy[2].wait()
 
 
-def merge(grad, error):
+def merge(grad, error, q_warm):
     _, rows, col_count = grad.shape
     return pl.pallas_call(
         merge_kernel,
-        out_shape=shape(BF16, rows, col_count),
-        in_specs=[ANY, ANY],
-        out_specs=ANY,
+        out_shape=(shape(BF16, rows, col_count), shape(BF16, *q_warm.shape)),
+        in_specs=[ANY, ANY, ANY],
+        out_specs=[ANY, VMEM],
         scratch_shapes=[pltpu.VMEM((rows, col_count), BF16)] * 3
-        + [pltpu.SemaphoreType.DMA((2, len(CUTS))), pltpu.SemaphoreType.DMA((len(CUTS),))],
+        + [
+            pltpu.VMEM(q_warm.shape, F32),
+            pltpu.SemaphoreType.DMA((2, len(CUTS))),
+            pltpu.SemaphoreType.DMA((len(CUTS),)),
+            pltpu.SemaphoreType.DMA,
+        ],
         compiler_params=pltpu.CompilerParams(vmem_limit_bytes=60 * 1024 * 1024),
-    )(grad, error)
+    )(grad, error, q_warm)
 
 
 def fold(square):
@@ -335,10 +346,10 @@
     rows, col_count = grad.shape[1:]
     cols = col_count // REPLICAS
     part = rows // NEARS
-    merged = merge(grad, error)
+    merged, warm = merge(grad, error, q_warm)
 
     landed = lax.all_to_all(merged.reshape(NEARS, part, col_count), NEAR, 0, 0)
-    warm = lax.all_gather(q_warm.astype(BF16), FSDP, axis=1, tiled=True)
+    warm = lax.all_gather(warm, FSDP, axis=1, tiled=True)
     shares = call(left_kernel, shape(BF16, REPLICAS, 2 * part, cols), landed, warm)
     shares = lax.all_to_all(shares, DP, 0, 0)
     means = call(mean_kernel, shape(F32, NEARS, part + part // 2, cols), shares)

time: 97.1 us -> 97.5 us (level)
  no operation moved by 1% of the time
where the time goes in v10:
time: 97.5 us; the launch traced here: 97.2 us
  blocking collectives  82.6 us (85%)
  Pallas kernels  8.02 us (8%)
  starting transfers between devices  5.87 us (6%)
    all_gather x1, blocking collectives, on_device(): warm = lax.all_gather(warm, FSDP, axis=1, tiled=True)  25.4 us
    all_to_all x1, blocking collectives, on_device(): shares = lax.all_to_all(shares, DP, 0, 0)  20.9 us
    all_to_all x1, blocking collectives, on_device(): q_all = lax.all_gather(lax.all_to_all(q_copies, DP, 0, 0), 'core')  13.8 us
    all_to_all x1, blocking collectives, on_device(): terms = lax.all_to_all(terms, 'z', 0, 0)  13.7 us
    all_to_all x1, starting transfers between devices, on_device(): landed = lax.all_to_all(merged.reshape(NEARS, part, col_count), NEAR, 0, 0)  5.87 us
    all_gather x1, blocking collectives, on_device(): q_all = lax.all_gather(lax.all_to_all(q_copies, DP, 0, 0), 'core')  5.09 us
    all_gather x1, blocking collectives, on_device(): lax.all_gather(means, 'core')  3.73 us
    pallas_call x4, Pallas kernels, call(): pl.pallas_call(kernel, out_shape=out, in_specs=[VMEM] * len(operands), ou...  3.67 us
  transfers between devices with their start and end apart: 1, of which 0 were waited for; matrix products, arithmetic and copies ran while one was open for 0% of the time, Pallas kernels for 0%

profile of v10, /device:TPU:1, one launch (start us, length us, event | category | flops | bytes accessed | tf_op | source)
XLA Modules:
  0.0 97.2 jit_solution(16027736827719786545)
XLA Ops:
  0.6 3.0 %shard_map.58 = (bf16[128,4096]{1,0:T(8,128)(2,1)}, bf16[64,256]{1,0:T(8,128)(2,1)}) custom-call(bf16[1,128,4096]{2,1,0:T(8,128)(2,1)} %grad_hbm.1, bf16[1,128,4096]{2,1,0:T(8,128)(2,1)} %error_hbm.1, f32[64,256]{1,0:T(8,128)} %q_hbm.1), custom_call_target="tpu_custom_call" | custom-call | tf_op jit(solution)/shard_map/pallas_call | solution.py:80
  3.6 0.0 copy-start.1
  3.6 5.9 %all-to-all-start = ((bf16[8,16,4096]{2,1,0:T(8,128)(2,1)}), bf16[8,16,4096]{2,1,0:T(8,128)(2,1)S(1)}, u32[]{:S(2)}, u32[]{:S(2)}) async-start(bf16[8,16,4096]{2,1,0:T(8,128)(2,1)} %bitcast.3), calls=%async_computation | async-start | bytes 2097152 | tf_op jit(solution)/shard_map/all_to_all | solution.py:351
  9.5 0.0 copy-done.1
  9.5 25.4 %all_gather.15.warm_ref = bf16[64,4096]{1,0:T(8,128)(2,1)S(1)} all-gather(bf16[64,256]{1,0:T(8,128)(2,1)S(1)} %copy-done.1), channel_id=1, replica_groups=mesh['yh'=4,'yl'=2,'x'=4,'z'=8,'core'=2] {'z','core'}, dimensions={1}, use_global_device_ids=true | all-gather | bytes 557056 | tf_op jit(solution)/shard_map/all_gather | solution.py:352
  34.9 0.0 all-to-all-done.landed_ref
  34.9 0.7 shard_map.59
  35.6 20.9 %all_to_all.20.landed_ref = bf16[32,32,128]{2,1,0:T(8,128)(2,1)S(1)} all-to-all(bf16[32,32,128]{2,1,0:T(8,128)(2,1)S(1)} %shard_map.59), channel_id=1, replica_groups=mesh['yh'=4,'yl'=2,'x'=4,'z'=8,'core'=2] {'yh','yl','x'}, dimensions={0} | all-to-all | bytes 524288 | tf_op jit(solution)/shard_map/all_to_all | solution.py:354
  56.5 0.2 shard_map.60
  56.7 3.7 %all-gather = f32[16,24,128]{2,1,0:T(8,128)S(1)} all-gather(f32[8,24,128]{2,1,0:T(8,128)S(1)} %shard_map.60), channel_id=2, replica_groups=mesh['yh'=4,'yl'=2,'x'=4,'z'=8,'core'=2] {'core'}, dimensions={0}, use_global_device_ids=true | all-gather | bytes 294912 | tf_op jit(solution)/shard_map/all_gather | solution.py:359
  60.4 0.5 shard_map.61
  60.9 0.0 copy-start
  60.9 13.7 %all_to_all.21.landed_ref = f32[8,56,128]{2,1,0:T(8,128)S(1)} all-to-all(f32[8,56,128]{2,1,0:T(8,128)S(1)} %get-tuple-element.11), channel_id=1, replica_groups=mesh['yh'=4,'yl'=2,'x'=4,'z'=8,'core'=2] {'z'}, dimensions={0} | all-to-all | bytes 458752 | tf_op jit(solution)/shard_map/all_to_all | solution.py:361
  74.5 2.4 %shard_map.62 = (bf16[32,32,128]{2,1,0:T(8,128)(2,1)S(1)}, bf16[128,64]{1,0:T(8,128)(2,1)S(1)}) custom-call(f32[8,56,128]{2,1,0:T(8,128)S(1)} %all_to_all.21.landed_ref, f32[128,64]{1,0:T(8,128)S(1)} %get-tuple-element.12.left_ref), custom_call_target="tpu_custom_call" | custom-call | tf_op jit(solution)/shard_map/pallas_call | solution.py:34
  76.9 13.8 %all_to_all.22 = bf16[32,32,128]{2,1,0:T(8,128)(2,1)S(1)} all-to-all(bf16[32,32,128]{2,1,0:T(8,128)(2,1)S(1)} %get-tuple-element.13), channel_id=1, replica_groups=mesh['yh'=4,'yl'=2,'x'=4,'z'=8,'core'=2] {'yh','yl','x'}, dimensions={0} | all-to-all | bytes 524288 | tf_op jit(solution)/shard_map/all_to_all | solution.py:369
  90.7 5.1 %all-gather.1 = bf16[64,32,128]{2,1,0:T(8,128)(2,1)S(1)} all-gather(bf16[32,32,128]{2,1,0:T(8,128)(2,1)S(1)} %all_to_all.22), channel_id=3, replica_groups=mesh['yh'=4,'yl'=2,'x'=4,'z'=8,'core'=2] {'core'}, dimensions={0}, use_global_device_ids=true | all-gather | bytes 786432 | tf_op jit(solution)/shard_map/all_gather | solution.py:369
  95.8 0.0 copy-done
  95.8 1.4 %shard_map.63 = (bf16[1,128,4096]{2,1,0:T(8,128)(2,1)}, bf16[128,128]{1,0:T(8,128)(2,1)}, f32[64,256]{1,0:T(8,128)}) custom-call(bf16[2,32,32,128]{3,2,1,0:T(8,128)(2,1)S(1)} %bitcast.4, bf16[128,64]{1,0:T(8,128)(2,1)S(1)} %get-tuple-element.14.ortho_ref, bf16[128,4096]{1,0:T(8,128)(2,1)S(1)} %copy-done), custom_call_target="tpu_custom_call" | custom-call | tf_op jit(solution)/shard_map/pallas_call | solution.py:324
Async XLA Ops:
  3.6 5.9 %copy-start.1 = (bf16[64,256]{1,0:T(8,128)(2,1)S(1)}, bf16[64,256]{1,0:T(8,128)(2,1)}, u32[]{:S(2)}) copy-start(bf16[64,256]{1,0:T(8,128)(2,1)} %get-tuple-element.10) | copy-start | bytes 98308
  3.6 31.3 %all-to-all-start = ((bf16[8,16,4096]{2,1,0:T(8,128)(2,1)}), bf16[8,16,4096]{2,1,0:T(8,128)(2,1)S(1)}, u32[]{:S(2)}, u32[]{:S(2)}) async-start(bf16[8,16,4096]{2,1,0:T(8,128)(2,1)} %bitcast.3), calls=%async_computation | async-start | bytes 2097152 | tf_op jit(solution)/shard_map/all_to_all | solution.py:351
  60.9 35.0 %copy-start = (bf16[128,4096]{1,0:T(8,128)(2,1)S(1)}, bf16[128,4096]{1,0:T(8,128)(2,1)}, u32[]{:S(2)}) copy-start(bf16[128,4096]{1,0:T(8,128)(2,1)} %get-tuple-element.9.merged) | copy-start | bytes 3145732
